TPU v7x, 256 devices: a whole 4x4x8 slice. The times are simulated.
256 devices in a mesh: img: 64 (over x_lo, y, z), tok: 4 (over x_hi, core).
Axes of the slice: x: 4 (x_hi: 2, x_lo: 2; x = x_hi * 2 + x_lo), y: 4, z: 8, core: 2. Of those that a mesh axis runs over, the one named last changes fastest.
Arguments:
- residuals: float32 [64, 32, 265], P('img', 'tok'), may hold values from -6 to 6
- stream: bfloat16 [64, 544, 1024], P('img', 'tok'), may hold values from -6 to 6
- token_slot: int32 [64, 521], P('img'), may hold values from 0 to 543, as said below
- level_embed: bfloat16 [7, 1024], replicated, may hold values from -3 to 3
- embed_weight: bfloat16 [32, 1024], replicated, may hold values from -1 to 1
- norm_gain: float32 [1024], replicated, may hold values from 0.1 to 1.9
- qkv_weight: bfloat16 [1024, 3072], replicated, may hold values from -2.5 to 2.5
- out_weight: bfloat16 [1024, 1024], replicated, may hold values from -0.1875 to 0.1875
- out_grad: bfloat16 [64, 544, 1024], P('img', 'tok'), may hold values from -0.625 to 0.625
Outputs:
- block_out: bfloat16 [64, 544, 1024], P('img', 'tok')
- qkv_weight_grad: float32 [1024, 3, 1024], P('img', None, 'tok')
- out_weight_grad: float32 [1024, 1024], P('img', 'tok')
Inputs may be any that keep to these rules, and one draw needn't show every extreme that they name: `token_slot`: within an image the slots are distinct; the token in slot t is held by tok index t // 136; the last slot is always taken.
All inputs are finite; a program needn't handle non-finite values.
Results may differ from a plain program's by a relative error of at most 0.024.
Values may be sent and summed in bfloat16 or wider, within the bound.
A program may use at most 128 MiB of HBM per device.

v0:
```python
import jax
import jax.numpy as jnp
import numpy as np
from jax import lax
from jax.sharding import PartitionSpec as P

HEADS = 8
HEAD_DIM = 128
NSCALE = 7


scale_sides = (1, 2, 4, 6, 8, 12, 16, 20)


def line_matrix(source, target):
    places = np.arange(target)
    numerator = (2 * places + 1) * source - target
    low_index = numerator // (2 * target)
    fraction = (numerator - low_index * 2 * target) / (2.0 * target)
    fraction = np.where(numerator < 0, 0.0, fraction)
    low_index = np.maximum(low_index, 0)
    fraction = np.where(low_index >= source - 1, 0.0, fraction)
    low_index = np.minimum(low_index, source - 1)
    high_index = np.minimum(low_index + 1, source - 1)
    columns = np.arange(source)
    return (columns[None, :] == low_index[:, None]) * (1.0 - fraction[:, None]) + (
        columns[None, :] == high_index[:, None]
    ) * fraction[:, None]


def token_scales():
    grid_sides = scale_sides[:NSCALE]
    return np.repeat(np.arange(NSCALE), [grid_side * grid_side for grid_side in grid_sides]).astype(
        np.int32
    )


def teacher_maps(residuals):
    grid_sides = scale_sides[:NSCALE]
    finest = grid_sides[-1]
    leading = residuals.shape[:-1]
    canvas = jnp.zeros(leading + (finest, finest), residuals.dtype)
    pieces = [jnp.zeros(leading + (1,), residuals.dtype)]
    offset = 0
    for scale_level in range(NSCALE - 1):
        grid_side = grid_sides[scale_level]
        block_map = residuals[..., offset : offset + grid_side * grid_side].reshape(
            leading + (grid_side, grid_side)
        )
        offset = offset + grid_side * grid_side
        upward = jnp.asarray(line_matrix(grid_side, finest), residuals.dtype)
        canvas = canvas + jnp.einsum(
            "ia,...ab,jb->...ij", upward, block_map, upward, precision=lax.Precision.HIGHEST
        )
        next_side = grid_sides[scale_level + 1]
        downward = jnp.asarray(line_matrix(finest, next_side), residuals.dtype)
        coarse = jnp.einsum(
            "ia,...ab,jb->...ij", downward, canvas, downward, precision=lax.Precision.HIGHEST
        )
        pieces.append(coarse.reshape(leading + (next_side * next_side,)))
    return jnp.concatenate(pieces, axis=-1)


def weight_terms(normed_rows, upstream_rows, query_cols, pair_cols, attended_cols):
    query_part = jnp.einsum(
        "isd,ise->de", normed_rows, query_cols, preferred_element_type=jnp.float32
    )
    pair_part = jnp.einsum(
        "isd,ispe->dpe", normed_rows.astype(jnp.float32), pair_cols, precision=lax.Precision.HIGHEST
    )
    out_part = jnp.einsum(
        "isd,ise->de", upstream_rows, attended_cols, preferred_element_type=jnp.float32
    )
    return jnp.concatenate([query_part[:, None, :], pair_part, out_part[:, None, :]], axis=1)


def per_device(
    residuals,
    stream,
    token_slot,
    level_embed,
    embed_weight,
    norm_gain,
    qkv_weight,
    out_weight,
    out_grad,
):
    groups = lax.axis_size("tok")
    member = lax.axis_index("tok")
    images, slot_count, width = out_grad.shape
    all_slots = groups * slot_count
    width_attn = HEADS * HEAD_DIM
    factor = HEAD_DIM ** (-0.5)
    scale_ids = jnp.asarray(token_scales())

    def slot_scales(slot_row):
        return jnp.full((all_slots,), NSCALE, jnp.int32).at[slot_row].set(scale_ids)

    slot_scale = jax.vmap(slot_scales)(token_slot)
    teacher = teacher_maps(residuals).astype(jnp.bfloat16)
    channels_here = teacher.shape[1]

    def spread(slot_row, maps):
        return jnp.zeros((channels_here, all_slots), jnp.bfloat16).at[:, slot_row].set(maps)

    arranged = jax.vmap(spread)(token_slot, teacher).reshape(
        images, channels_here, groups, slot_count
    )
    moved = lax.all_to_all(arranged, "tok", split_axis=2, concat_axis=1, tiled=True)
    local_inputs = moved.reshape(images, channels_here * groups, slot_count)
    own_scale = lax.dynamic_slice_in_dim(slot_scale, member * slot_count, slot_count, 1)
    valid = own_scale < NSCALE
    onehot = (own_scale[..., None] == jnp.arange(NSCALE, dtype=jnp.int32)).astype(jnp.float32)
    level_terms = jnp.einsum(
        "isn,nd->isd", onehot, level_embed.astype(jnp.float32), precision=lax.Precision.HIGHEST
    )
    embedded = jnp.einsum(
        "ics,cd->isd", local_inputs, embed_weight, preferred_element_type=jnp.float32
    )
    block_in = (embedded + level_terms + stream.astype(jnp.float32)).astype(jnp.bfloat16)
    values_in = block_in.astype(jnp.float32)
    normed = (
        values_in
        * lax.rsqrt(jnp.mean(values_in * values_in, axis=-1, keepdims=True) + 1e-06)
        * norm_gain
    ).astype(jnp.bfloat16)
    projected = jnp.einsum(
        "isd,de->ise", normed, qkv_weight, preferred_element_type=jnp.float32
    ).astype(jnp.bfloat16)
    queries = projected[..., :width_attn]
    pair_local = projected[..., width_attn:]
    pair_all = lax.all_gather(pair_local, "tok", axis=1, tiled=True)
    query_heads = queries.reshape(images, slot_count, HEADS, HEAD_DIM)
    key_heads = pair_all[..., :width_attn].reshape(images, all_slots, HEADS, HEAD_DIM)
    value_heads = pair_all[..., width_attn:].reshape(images, all_slots, HEADS, HEAD_DIM)
    scores = (
        jnp.einsum("iqhd,ikhd->ihqk", query_heads, key_heads, preferred_element_type=jnp.float32)
        * factor
    )
    allowed = slot_scale[:, None, None, :] <= own_scale[:, None, :, None]
    scores = jnp.where(allowed, scores, -jnp.inf)
    top = jnp.max(scores, axis=-1, keepdims=True)
    expd = jnp.exp(scores - top)
    total = jnp.sum(expd, axis=-1, keepdims=True)
    probs = (expd / total).astype(jnp.bfloat16)
    attended = (
        jnp.einsum("ihqk,ikhd->iqhd", probs, value_heads, preferred_element_type=jnp.float32)
        .reshape(images, slot_count, width_attn)
        .astype(jnp.bfloat16)
    )
    mixed = values_in + jnp.einsum(
        "ish,dh->isd", attended, out_weight, preferred_element_type=jnp.float32
    )
    block_out = jnp.where(valid[..., None], mixed, 0.0).astype(jnp.bfloat16)
    upstream = jnp.where(valid[..., None], out_grad, jnp.zeros_like(out_grad))
    attended_grad = jnp.einsum(
        "isd,dh->ish", upstream, out_weight, preferred_element_type=jnp.float32
    ).astype(jnp.bfloat16)
    grad_heads = attended_grad.reshape(images, slot_count, HEADS, HEAD_DIM)
    dprobs = jnp.einsum(
        "iqhd,ikhd->ihqk", grad_heads, value_heads, preferred_element_type=jnp.float32
    )
    delta = jnp.sum(probs.astype(jnp.float32) * dprobs, axis=-1, keepdims=True)
    score_grad = (probs.astype(jnp.float32) * (dprobs - delta) * factor).astype(jnp.bfloat16)
    query_grad = (
        jnp.einsum("ihqk,ikhd->iqhd", score_grad, key_heads, preferred_element_type=jnp.float32)
        .astype(jnp.bfloat16)
        .reshape(images, slot_count, width_attn)
    )
    log_total = top[..., 0] + jnp.log(total[..., 0])
    far_queries, far_grads, far_logs, far_delta = (
        lax.all_gather(queries.astype(jnp.float32), "tok", axis=1, tiled=True).astype(
            queries.dtype
        ),
        lax.all_gather(attended_grad.astype(jnp.float32), "tok", axis=1, tiled=True).astype(
            attended_grad.dtype
        ),
        lax.all_gather(log_total, "tok", axis=2, tiled=True),
        lax.all_gather(delta[..., 0], "tok", axis=2, tiled=True),
    )
    own_key_heads = pair_local[..., :width_attn].reshape(images, slot_count, HEADS, HEAD_DIM)
    own_value_heads = pair_local[..., width_attn:].reshape(images, slot_count, HEADS, HEAD_DIM)
    far_query_heads = far_queries.reshape(images, all_slots, HEADS, HEAD_DIM)
    far_grad_heads = far_grads.reshape(images, all_slots, HEADS, HEAD_DIM)
    far_scores = (
        jnp.einsum(
            "iqhd,ikhd->ihqk", far_query_heads, own_key_heads, preferred_element_type=jnp.float32
        )
        * factor
    )
    far_allowed = own_scale[:, None, None, :] <= slot_scale[:, None, :, None]
    far_probs = jnp.where(far_allowed, jnp.exp(far_scores - far_logs[..., None]), 0.0).astype(
        jnp.bfloat16
    )
    far_dprobs = jnp.einsum(
        "iqhd,ikhd->ihqk", far_grad_heads, own_value_heads, preferred_element_type=jnp.float32
    )
    far_score_grad = (
        far_probs.astype(jnp.float32) * (far_dprobs - far_delta[..., None]) * factor
    ).astype(jnp.bfloat16)
    key_grad = jnp.einsum(
        "ihqk,iqhd->ikhd", far_score_grad, far_query_heads, preferred_element_type=jnp.float32
    )
    value_grad = jnp.einsum(
        "ihqk,iqhd->ikhd", far_probs, far_grad_heads, preferred_element_type=jnp.float32
    )
    pair_grad = jnp.concatenate(
        [
            key_grad.reshape(images, slot_count, width_attn),
            value_grad.reshape(images, slot_count, width_attn),
        ],
        axis=-1,
    )
    pair_grad = pair_grad.reshape(images, slot_count, 2, width_attn)
    normed_all, upstream_all = (
        lax.all_gather(normed, "tok", axis=1, tiled=True),
        lax.all_gather(upstream, "tok", axis=1, tiled=True),
    )
    query_cols, attended_cols = (
        lax.all_to_all(
            query_grad.reshape(images, slot_count, 1, width_attn),
            "tok",
            split_axis=3,
            concat_axis=1,
            tiled=True,
        ),
        lax.all_to_all(
            attended.reshape(images, slot_count, 1, width_attn),
            "tok",
            split_axis=3,
            concat_axis=1,
            tiled=True,
        ),
    )
    pair_cols = lax.all_to_all(
        pair_grad.astype(jnp.bfloat16), "tok", split_axis=3, concat_axis=1, tiled=True
    ).astype(pair_grad.dtype)
    combined = lax.psum_scatter(
        weight_terms(
            normed_all, upstream_all, query_cols[:, :, 0, :], pair_cols, attended_cols[:, :, 0, :]
        ),
        "img",
        scatter_dimension=0,
        tiled=True,
    )
    return (block_out, combined[:, :3, :], combined[:, 3, :])


def solution(mesh):
    in_specs = (
        P("img", "tok", None),
        P("img", "tok", None),
        P("img", None),
        P(),
        P(),
        P(),
        P(),
        P(),
        P("img", "tok", None),
    )
    out_specs = (P("img", "tok", None), P("img", None, "tok"), P("img", "tok"))
    return jax.shard_map(
        per_device, mesh=mesh, in_specs=in_specs, out_specs=out_specs, check_vma=False
    )
```

profile of v0, /device:TPU:2, one launch (start us, length us, event | category | flops | bytes accessed | tf_op | source)
XLA Modules:
  0.0 545.2 jit_solution(2790522445650575508)
XLA Ops:
  25.4 4.2 scatter_custom_fusion.1
  30.4 3.4 all-to-all-start
  33.8 4.3 scatter_custom_fusion
  40.8 3.9 fusion
  51.8 20.2 %all-gather.15.cloned.1.call-done = bf16[1,544,1024]{2,1,0:T(8,128)(2,1)} async-done(((bf16[1,136,1024]{2,1,0:T(8,128)(2,1)}), bf16[1,544,1024]{2,1,0:T(8,128)(2,1)}) %all-gather.15.cloned.1.call-update) | async-done | bytes 1114128 | tf_op jit(solution)/shard_map/all_gather | solution.py:172
  74.6 28.7 %all-gather.11.cloned.1.call-done = bf16[1,544,2048]{2,1,0:T(8,128)(2,1)} async-done(((bf16[1,136,2048]{2,1,0:T(8,128)(2,1)}), bf16[1,544,2048]{2,1,0:T(8,128)(2,1)}) %all-gather.11.cloned.1.call-update) | async-done | bytes 2228240 | tf_op jit(solution)/shard_map/all_gather | solution.py:132
  113.9 4.2 reshape.662
  118.6 5.7 %reduce.12 = bf16[1024,136]{1,0:T(8,128)(2,1)} reduce(bf16[1024,1,1,136]{3,2,1,0:T(2,128)(2,1)} %bitcast.259, bf16[]{:T(256)} %broadcast.179), dimensions={1,2}, to_apply=%bitcast.193.reduce_sub_computation | reduce | bytes 557058
  124.3 2.9 reshape.672
  127.1 4.1 all-to-all-start.1
  131.2 8.7 %all-gather.3 = f32[4,136,8]{1,2,0:T(8,128)S(1)} all-gather(f32[1,136,8]{1,2,0:T(8,128)S(1)} %add_bitcast_fusion), channel_id=2, replica_groups=mesh['img'=64,'tok'=4] {'tok'}, dimensions={0}, use_global_device_ids=true | all-gather | bytes 21760 | tf_op jit(solution)/shard_map/all_gather | solution.py:178
  140.7 6.9 %all-gather.4 = f32[4,136,8]{1,2,0:T(8,128)S(1)} all-gather(f32[1,136,8]{1,2,0:T(8,128)S(1)} %bitcast.280), channel_id=4, replica_groups=mesh['img'=64,'tok'=4] {'tok'}, dimensions={0}, use_global_device_ids=true | all-gather | bytes 21760 | tf_op jit(solution)/shard_map/all_gather | solution.py:179
  152.2 3.4 reshape.663
  155.6 4.8 reduce.11
  160.5 2.9 reshape.670
  165.8 3.9 fusion.29
  169.6 4.1 all-to-all-start.3
  173.8 2.6 fusion.28
  179.8 3.1 reshape.673
  184.4 4.7 all-to-all-start.2
  189.2 4.0 reshape.671
  197.4 2.9 convolution_bitcast_fusion.1
  200.3 2.9 convolution_bitcast_fusion
  216.1 319.5 %reduce-scatter.2.cloned.1.call-done = f32[16,4,256]{2,0,1:T(8,128)} async-done(((f32[1024,4,256]{2,0,1:T(8,128)}), f32[16,4,256]{2,0,1:T(8,128)}) %reduce-scatter.2.cloned.1.call-update) | async-done | bytes 65552 | tf_op jit(solution)/shard_map/reduce_scatter | solution.py:238
  (174 shorter events, 74.5 us)
Async XLA Ops:
  7.2 39.7 %copy-start = (bf16[1024,1024]{1,0:T(8,128)(2,1)S(1)}, bf16[1024,1024]{1,0:T(8,128)(2,1)}, u32[]{:S(2)}) copy-start(bf16[1024,1024]{1,0:T(8,128)(2,1)} %param.29) | copy-start | bytes 6291460
  7.2 14.8 %copy-start.18 = (f32[16,16,1]{1,0,2:T(8,128)S(1)}, f32[16,16,1]{1,0,2:T(8,128)}, u32[]{:S(2)}) copy-start(f32[16,16,1]{1,0,2:T(8,128)} %constant.92) | copy-start | bytes 3076
  7.2 15.3 %copy-start.17 = (f32[12,16,1]{1,0,2:T(8,128)S(1)}, f32[12,16,1]{1,0,2:T(8,128)}, u32[]{:S(2)}) copy-start(f32[12,16,1]{1,0,2:T(8,128)} %constant.90) | copy-start | bytes 2308
  7.2 15.8 %copy-start.22 = (f32[8,16,1]{1,0,2:T(8,128)S(1)}, f32[8,16,1]{1,0,2:T(8,128)}, u32[]{:S(2)}) copy-start(f32[8,16,1]{1,0,2:T(8,128)} %constant.88) | copy-start | bytes 1540
  7.2 16.3 %copy-start.21 = (f32[6,16,1]{1,0,2:T(8,128)S(1)}, f32[6,16,1]{1,0,2:T(8,128)}, u32[]{:S(2)}) copy-start(f32[6,16,1]{1,0,2:T(8,128)} %constant.86) | copy-start | bytes 1156
  7.2 16.7 %copy-start.23 = (f32[4,16,1]{1,0,2:T(4,128)S(1)}, f32[4,16,1]{1,0,2:T(4,128)}, u32[]{:S(2)}) copy-start(f32[4,16,1]{1,0,2:T(4,128)} %constant.84) | copy-start | bytes 772
  7.2 17.2 %copy-start.26 = (f32[2,16,1]{1,0,2:T(2,128)S(1)}, f32[2,16,1]{1,0,2:T(2,128)}, u32[]{:S(2)}) copy-start(f32[2,16,1]{1,0,2:T(2,128)} %constant.82) | copy-start | bytes 388
  7.3 18.1 %copy-start.25 = (s32[1,521]{1,0:T(1,128)S(1)}, s32[1,521]{1,0:T(1,128)}, u32[]{:S(2)}) copy-start(s32[1,521]{1,0:T(1,128)} %param.24) | copy-start | bytes 6256
  12.6 26.5 %copy-start.16 = (bf16[32,1024]{1,0:T(8,128)(2,1)S(1)}, bf16[32,1024]{1,0:T(8,128)(2,1)}, u32[]{:S(2)}) copy-start(bf16[32,1024]{1,0:T(8,128)(2,1)} %param.26) | copy-start | bytes 196612
  19.1 20.2 %copy-start.14 = (bf16[1,136,1024]{2,1,0:T(8,128)(2,1)S(1)}, bf16[1,136,1024]{2,1,0:T(8,128)(2,1)}, u32[]{:S(2)}) copy-start(bf16[1,136,1024]{2,1,0:T(8,128)(2,1)} %param.23) | copy-start | bytes 835588
  19.1 20.2 %copy-start.20 = (bf16[7,1024]{1,0:T(8,128)(2,1)S(1)}, bf16[7,1024]{1,0:T(8,128)(2,1)}, u32[]{:S(2)}) copy-start(bf16[7,1024]{1,0:T(8,128)(2,1)} %param.25) | copy-start | bytes 43012
  23.8 16.9 %copy-start.24 = (f32[1024]{0:T(1024)S(1)}, f32[1024]{0:T(1024)}, u32[]{:S(2)}) copy-start(f32[1024]{0:T(1024)} %param.27) | copy-start | bytes 12292
  30.4 8.8 %all-to-all-start = ((bf16[1,8,4,136]{3,1,0,2:T(8,128)(2,1)}), bf16[1,8,4,136]{3,1,0,2:T(8,128)(2,1)S(1)}, u32[]{:S(2)}, u32[]{:S(2)}) async-start(bf16[1,8,4,136]{3,1,0,2:T(8,128)(2,1)} %copy.130), calls=%async_computation | async-start | bytes 32768 | tf_op jit(solution)/shard_map/all_to_all | solution.py:109
  33.8 38.2 %all-gather.15.cloned.1.call-start = ((), (), s32[]{:S(2)}) async-start(), calls=%async_computation.7 | async-start | bytes 1392640 | tf_op jit(solution)/shard_map/all_gather | solution.py:172
  45.7 57.5 %all-gather.11.cloned.1.call-start = ((), (), s32[]{:S(2)}) async-start(), calls=%async_computation.5 | async-start | bytes 2785280 | tf_op jit(solution)/shard_map/all_gather | solution.py:132
  46.7 119.0 %all-gather.19.cloned.1.call-start = ((), (), s32[]{:S(2)}) async-start(), calls=%async_computation.10 | async-start | bytes 1392640 | tf_op jit(solution)/shard_map/all_gather | solution.py:175
  48.1 149.3 %all-gather.13.cloned.1.call-start = ((), (), s32[]{:S(2)}) async-start(), calls=%async_computation.6 | async-start | bytes 1392640 | tf_op jit(solution)/shard_map/all_gather | solution.py:216
  48.7 151.6 %all-gather.17.cloned.1.call-start = ((), (), s32[]{:S(2)}) async-start(), calls=%async_computation.8 | async-start | bytes 1392640 | tf_op jit(solution)/shard_map/all_gather | solution.py:217
  49.4 57.5 %copy-start.12 = (pred[136,544]{1,0:T(8,128)(4,1)}, pred[136,544]{1,0:T(8,128)(4,1)S(1)}, u32[]{:S(2)}) copy-start(pred[136,544]{1,0:T(8,128)(4,1)S(1)} %broadcast_compare_fusion) | copy-start | bytes 221956
  127.1 42.5 %all-to-all-start.1 = ((bf16[4,2,17408]{2,1,0:T(2,128)(2,1)}), bf16[4,2,17408]{2,1,0:T(2,128)(2,1)}, u32[]{:S(2)}, u32[]{:S(2)}) async-start(bf16[4,2,17408]{2,1,0:T(2,128)(2,1)} %reshape.672), calls=%async_computation.1 | async-start | bytes 557056 | tf_op jit(solution)/shard_map/all_to_all | solution.py:220
  155.6 7.7 %copy-start.19 = (f32[544,8]{0,1:T(8,128)S(1)}, f32[544,8]{0,1:T(8,128)}, u32[]{:S(2)}) copy-start(f32[544,8]{0,1:T(8,128)} %reshape.643) | copy-start | bytes 52228
  169.6 14.8 %all-to-all-start.3 = ((bf16[4,2,17408]{2,1,0:T(2,128)(2,1)}), bf16[4,2,17408]{2,1,0:T(2,128)(2,1)}, u32[]{:S(2)}, u32[]{:S(2)}) async-start(bf16[4,2,17408]{2,1,0:T(2,128)(2,1)} %reshape.670), calls=%async_computation.3 | async-start | bytes 557056 | tf_op jit(solution)/shard_map/all_to_all | solution.py:227
  184.4 20.7 %all-to-all-start.2 = ((bf16[1,136,2,1024]{1,2,0,3:T(2,128)(2,1)}), bf16[1,136,2,1024]{1,2,0,3:T(2,128)(2,1)S(1)}, u32[]{:S(2)}, u32[]{:S(2)}) async-start(bf16[1,136,2,1024]{1,2,0,3:T(2,128)(2,1)} %copy.152), calls=%async_computation.2 | async-start | bytes 2097152 | tf_op jit(solution)/shard_map/all_to_all | solution.py:235
  189.2 346.4 %reduce-scatter.2.cloned.1.call-start = ((), (), s32[]{:S(2)}) async-start(), calls=%async_computation.9 | async-start | bytes 4259840 | tf_op jit(solution)/shard_map/reduce_scatter | solution.py:238
  (13 other events, 25.1 us)
Sparse Core Ops, SparseCore 0:
  45.9 26.1 all-gather.14
  73.8 29.3 all-gather.10
  105.1 23.1 all-gather.18
  129.9 23.3 all-gather.12
  154.9 23.1 all-gather.16
  213.6 321.9 reduce-scatter.1
where the time goes:
time: 548 us; the launch traced here: 545 us
  waiting for transfers between devices  372 us (68%)
  local copies, waits for them, and re-layouts  67.3 us (12%)
  matrix products  43.6 us (8%)
  starting transfers between devices  16.7 us (3%)
  blocking collectives  15.6 us (3%)
  other arithmetic  14.9 us (3%)
  between operations  14.8 us (3%)
    reduce_scatter x1, waiting for transfers between devices, per_device(): lax.psum_scatter(weight_terms(normed_all, upstream_all, query_cols[:, :,...  319 us
    all_gather x1, waiting for transfers between devices, per_device(): pair_all = lax.all_gather(pair_local, 'tok', axis=1, tiled=True)  28.7 us
    unnamed x70, local copies, waits for them, and re-layouts  24 us
    all_gather x1, waiting for transfers between devices, per_device(): lax.all_gather(queries.astype(jnp.float32), 'tok', axis=1, tiled=True)  20.2 us
  transfers between devices with their start and end apart: 10, of which 5 were waited for; matrix products, arithmetic and copies ran while one was open for 15% of the time, Pallas kernels for 0%

commit v1 on v0

v1 whole, which is shorter than its diff:
```python
import functools

import jax
import jax.numpy as jnp
import numpy as np
from jax import lax
from jax.experimental import pallas as pl
from jax.experimental.pallas import tpu as pltpu
from jax.sharding import PartitionSpec as P

D = 1024
HEAD_DIM = 128
NSCALE = 7
SLOT = 136
PAD = 144
CHUNK = 48
SLABS = 4
ROWS = SLABS * PAD
COLS = 256
SIDES = (1, 2, 4, 6, 8, 12, 16)
TOK_IMG = 521
TOK_IN = 265
SIZE = {"x": 2, "y": 4, "z": 8}
BLOCKS = ("out", "v", "q", "k")
ORDER = {"out": "yxz", "v": "xyz", "q": "yxz", "k": "xyz"}
PLACE = {"q": 0, "k": 1, "v": 2}
MESH = pl.DeviceIdType.MESH
F32 = jnp.float32
BF16 = jnp.bfloat16


def line_matrix(source, target):
    places = np.arange(target)
    numerator = (2 * places + 1) * source - target
    low_index = numerator // (2 * target)
    fraction = (numerator - low_index * 2 * target) / (2.0 * target)
    fraction = np.where(numerator < 0, 0.0, fraction)
    low_index = np.maximum(low_index, 0)
    fraction = np.where(low_index >= source - 1, 0.0, fraction)
    low_index = np.minimum(low_index, source - 1)
    high_index = np.minimum(low_index + 1, source - 1)
    columns = np.arange(source)
    return (columns[None, :] == low_index[:, None]) * (1.0 - fraction[:, None]) + (
        columns[None, :] == high_index[:, None]
    ) * fraction[:, None]


def teacher_matrix():
    finest = SIDES[-1]
    starts = np.concatenate([[0], np.cumsum([s * s for s in SIDES])])
    whole = np.zeros((TOK_IMG, TOK_IN))
    for k in range(NSCALE - 1):
        down = line_matrix(finest, SIDES[k + 1])
        for j in range(k + 1):
            one = down @ line_matrix(SIDES[j], finest)
            whole[starts[k + 1] : starts[k + 2], starts[j] : starts[j + 1]] = np.kron(one, one)
    return whole.astype(np.float32)


def scale_tables():
    scale = np.repeat(np.arange(NSCALE), [s * s for s in SIDES])
    table = np.zeros((TOK_IMG, 8), np.float32)
    table[np.arange(TOK_IMG), scale] = 1.0
    table[:, 7] = scale - NSCALE
    row = np.zeros((8, TOK_IMG), np.float32)
    row[0] = scale - NSCALE
    return table, row


def dot(a, b, ca=1, cb=0, **kw):
    return lax.dot_general(
        a, b, (((ca,), (cb,)), ((), ())), preferred_element_type=F32, **kw
    )


def kernel(names, *refs):
    r = dict(zip(names, refs, strict=True))
    i, t = lax.axis_index("img"), lax.axis_index("tok")
    core, x_hi = lax.rem(t, 2), lax.div(t, 2)
    mine = {"x": lax.div(i, 32), "y": lax.rem(lax.div(i, 8), 4), "z": lax.rem(i, 8)}

    tok_of = [t, x_hi * 2 + (1 - core), (1 - x_hi) * 2 + core, (1 - x_hi) * 2 + (1 - core)]
    peer = [(i, n) for n in tok_of]

    def along(axis, d):
        at = dict(mine)
        at[axis] = lax.rem(mine[axis] + d, SIZE[axis])
        return ((at["x"] * 4 + at["y"]) * 8 + at["z"], t)

    send, recv = r["send"], r["recv"]
    used = [0]

    def remote(src, dst, device):
        n = used[0]
        used[0] += 1
        return pltpu.make_async_remote_copy(
            src_ref=src,
            dst_ref=dst,
            send_sem=send.at[n],
            recv_sem=recv.at[n],
            device_id=device,
            device_id_type=MESH,
        )

    loads = []
    for s in range(SLABS):
        at = pl.multiple_of(tok_of[s] * COLS, COLS)
        loads.append(
            pltpu.make_async_copy(
                r["out_weight"].at[:, pl.ds(at, COLS)], r["ow"].at[s], r["local"].at[s]
            )
        )
    for b in range(3):
        at = pl.multiple_of(b * D + t * COLS, COLS)
        loads.append(
            pltpu.make_async_copy(
                r["qkv_weight"].at[:, pl.ds(at, COLS)], r["wq"].at[b], r["local"].at[4 + b]
            )
        )
    for load in loads:
        load.start()

    friends = peer[1:] + [along(a, d) for a in "xyz" for d in range(1, SIZE[a])]
    barrier = pltpu.get_barrier_semaphore()
    for f in friends:
        pl.semaphore_signal(barrier, inc=1, device_id=f, device_id_type=MESH)

    none = jnp.zeros((PAD - SLOT, D), F32)
    r["res"][t] = r["residuals"][0]
    r["sbuf"][0] = jnp.concatenate([r["stream"][0].astype(F32), none], 0).astype(BF16)
    r["ubuf"][0] = jnp.concatenate([r["out_grad"][0].astype(F32), none], 0).astype(BF16)
    pl.semaphore_wait(barrier, len(friends))

    res_copies = [remote(r["res"].at[t], r["res"].at[t], peer[s]) for s in (1, 2, 3)]
    pieces = [pl.ds(CHUNK * c, CHUNK) for c in range(PAD // CHUNK)]

    def gather_copies(buf):
        cross = [remote(buf.at[0, p], buf.at[2, p], peer[2]) for p in pieces]
        near = remote(buf.at[0], buf.at[1], peer[1])
        onward = [remote(buf.at[2, p], buf.at[3, p], peer[1]) for p in pieces]
        return cross, near, onward

    s_cross, s_near, s_onward = gather_copies(r["sbuf"])
    u_cross, u_near, u_onward = gather_copies(r["ubuf"])
    for c in res_copies + s_cross + [s_near]:
        c.start()

    row = lax.broadcasted_iota(jnp.int32, (ROWS, 1), 0)
    slot = jnp.full((ROWS, 1), -1, jnp.int32)
    for s in range(SLABS):
        inside = (row >= s * PAD) & (row < s * PAD + SLOT)
        slot = jnp.where(inside, row + (tok_of[s] * SLOT - s * PAD), slot)
    pick = jnp.where(slot == r["token_slot"][...], 1.0, 0.0).astype(BF16)
    levels = dot(pick, r["scale_table"][...])
    sc_col = levels[:, 7:8]
    r["sc_col"][...] = sc_col
    r["sc_row"][...] = dot(r["scale_row"][...], pick, 1, 1)
    for c in res_copies:
        c.wait_recv()
    teacher = dot(
        r["teacher_map"][...],
        r["res"][...].reshape(32, TOK_IN),
        1,
        1,
        precision=lax.Precision.HIGHEST,
    ).astype(BF16)
    r["chan"][...] = dot(pick, teacher).astype(BF16)
    r["lev"][...] = levels[:, :7].astype(BF16)

    def enter(s):
        at = pl.ds(s * PAD, PAD)
        base = dot(r["chan"][at, :], r["embed_weight"][...]) + dot(
            r["lev"][at, :], r["level_embed"][...]
        )
        block_in = (base + r["sbuf"][s].astype(F32)).astype(BF16)
        if s == 0:
            r["block_in"][...] = block_in
        x = block_in.astype(F32)
        scale = lax.rsqrt(jnp.mean(x * x, axis=-1, keepdims=True) + 1e-6)
        r["normed"][at, :] = (x * scale * r["norm_gain"][...]).astype(BF16)

    def project(first):
        at = pl.ds(first * PAD, 2 * PAD)
        for b in range(3):
            r["qkv"][b, at, :] = dot(r["normed"][at, :], r["wq"][b]).astype(BF16)

    enter(0)
    s_near.wait_recv()
    enter(1)
    for load in loads:
        load.wait()
    project(0)
    for c in range(len(pieces)):
        s_cross[c].wait_recv()
        s_onward[c].start()
        u_cross[c].start()
    u_near.start()
    enter(2)
    for c in s_onward:
        c.wait_recv()
    enter(3)
    project(2)

    factor = HEAD_DIM ** (-0.5)
    heads = [slice(h * HEAD_DIM, (h + 1) * HEAD_DIM) for h in range(2)]
    for h in range(2):
        k, v = r["qkv"][1, :, heads[h]], r["qkv"][2, :, heads[h]]
        for s in range(SLABS):
            at = pl.ds(s * PAD, PAD)
            scores = dot(r["qkv"][0, at, heads[h]], k, 1, 1) * factor
            allowed = r["sc_row"][0:1, :] <= r["sc_col"][at, :]
            scores = jnp.where(allowed, scores, -jnp.inf)
            top = jnp.max(scores, axis=-1, keepdims=True)
            expd = jnp.exp(scores - top)
            total = jnp.sum(expd, axis=-1, keepdims=True)
            probs = (expd * (1.0 / total)).astype(BF16)
            r["probs"][h, at, :] = probs
            r["att"][s, :, heads[h]] = dot(probs, v).astype(BF16)

    a_copies = [remote(r["att"].at[s], r["attin"].at[s - 1], peer[s]) for s in (1, 2, 3)]
    for c in a_copies:
        c.start()

    for c in range(len(pieces)):
        u_cross[c].wait_recv()
        u_onward[c].start()
    u_near.wait_recv()
    for c in u_onward:
        c.wait_recv()
    for s in range(SLABS):
        at = pl.ds(s * PAD, PAD)
        up = jnp.where(r["sc_col"][at, :] < 0.0, r["ubuf"][s].astype(F32), 0.0)
        r["up"][at, :] = up.astype(BF16)

    sums = {}

    def first_stage(name, rows_ref, cols):
        order = ORDER[name]
        g = dot(r[rows_ref][...], cols, 0, 0)
        gf, gb = r["gf_" + name], r["gb_" + name]
        for x in range(2):
            for y in range(4):
                part = g[x * 512 + y * 128 : x * 512 + (y + 1) * 128].reshape(8, 16, COLS)
                at = tuple({"x": x, "y": y}[a] for a in order[:2])
                gf[at] = part
                gb[at] = part.astype(BF16)
        return start(name, 0, gb)

    def start(name, stage, src):
        axis = ORDER[name][stage]
        n = SIZE[axis]
        copies = [
            remote(
                src.at[lax.rem(mine[axis] + d, n)],
                r[f"r{stage}_{name}"].at[d - 1],
                along(axis, d),
            )
            for d in range(1, n)
        ]
        for c in copies:
            c.start()
        sums[name, stage] = copies

    def finish(name, stage):
        axis = ORDER[name][stage]
        own = r["gf_" + name] if stage == 0 else r[f"sf{stage - 1}_{name}"]
        for c in sums[name, stage]:
            c.wait_recv()
        total = own[mine[axis]]
        for d in range(1, SIZE[axis]):
            total = total + r[f"r{stage}_{name}"][d - 1].astype(F32)
        if stage < 2:
            r[f"sf{stage}_{name}"][...] = total
            r[f"sb{stage}_{name}"][...] = total.astype(BF16)
            start(name, stage + 1, r[f"sb{stage}_{name}"])
        elif name == "out":
            r["out_weight_grad"][...] = total
        else:
            r["qkv_weight_grad"][:, PLACE[name], :] = total

    att = jnp.concatenate([r["att"][s] for s in range(SLABS)], 0)
    first_stage("out", "up", att)
    r["ag"][...] = dot(r["up"][...], r["ow"][0]).astype(BF16)
    for h in range(2):
        r["dv"][:, heads[h]] = dot(r["probs"][h], r["ag"][:, heads[h]], 0, 0).astype(BF16)
    first_stage("v", "normed", r["dv"][...])
    for h in range(2):
        k, v = r["qkv"][1, :, heads[h]], r["qkv"][2, :, heads[h]]
        for s in range(SLABS):
            at = pl.ds(s * PAD, PAD)
            dprobs = dot(r["ag"][at, heads[h]], v, 1, 1)
            probs = r["probs"][h, at, :].astype(F32)
            delta = jnp.sum(probs * dprobs, axis=-1, keepdims=True)
            ds = (probs * (dprobs - delta) * factor).astype(BF16)
            r["ds"][h, at, :] = ds
            r["dq"][at, heads[h]] = dot(ds, k).astype(BF16)
    first_stage("q", "normed", r["dq"][...])
    for h in range(2):
        r["dk"][:, heads[h]] = dot(r["ds"][h], r["qkv"][0, :, heads[h]], 0, 0).astype(BF16)
    first_stage("k", "normed", r["dk"][...])
    finish("out", 0)

    mixed = r["block_in"][...].astype(F32) + dot(r["att"][0], r["ow"][0], 1, 1)
    for s in (1, 2, 3):
        a_copies[s - 1].wait_recv()
        mixed = mixed + dot(r["attin"][s - 1], r["ow"][s], 1, 1)
    mixed = jnp.where(r["sc_col"][pl.ds(0, PAD), :] < 0.0, mixed, 0.0)
    r["block_out"][0] = mixed[:SLOT].astype(BF16)

    for name in BLOCKS[1:]:
        finish(name, 0)
    for stage in (1, 2):
        for name in BLOCKS:
            finish(name, stage)
    for c in res_copies + s_cross + s_onward + u_cross + u_onward + a_copies + [s_near, u_near]:
        c.wait_send()
    for copies in sums.values():
        for c in copies:
            c.wait_send()


def scratch():
    out = {
        "send": pltpu.SemaphoreType.DMA((68,)),
        "recv": pltpu.SemaphoreType.DMA((68,)),
        "local": pltpu.SemaphoreType.DMA((7,)),
        "ow": pltpu.VMEM((SLABS, D, COLS), BF16),
        "wq": pltpu.VMEM((3, D, COLS), BF16),
        "res": pltpu.VMEM((4, 8, TOK_IN), F32),
        "sbuf": pltpu.VMEM((SLABS, PAD, D), BF16),
        "ubuf": pltpu.VMEM((SLABS, PAD, D), BF16),
        "sc_col": pltpu.VMEM((ROWS, 1), F32),
        "sc_row": pltpu.VMEM((8, ROWS), F32),
        "chan": pltpu.VMEM((ROWS, 32), BF16),
        "lev": pltpu.VMEM((ROWS, 7), BF16),
        "block_in": pltpu.VMEM((PAD, D), BF16),
        "normed": pltpu.VMEM((ROWS, D), BF16),
        "up": pltpu.VMEM((ROWS, D), BF16),
        "qkv": pltpu.VMEM((3, ROWS, COLS), BF16),
        "probs": pltpu.VMEM((2, ROWS, ROWS), BF16),
        "ds": pltpu.VMEM((2, ROWS, ROWS), BF16),
        "att": pltpu.VMEM((SLABS, PAD, COLS), BF16),
        "attin": pltpu.VMEM((SLABS - 1, PAD, COLS), BF16),
        "ag": pltpu.VMEM((ROWS, COLS), BF16),
        "dv": pltpu.VMEM((ROWS, COLS), BF16),
        "dq": pltpu.VMEM((ROWS, COLS), BF16),
        "dk": pltpu.VMEM((ROWS, COLS), BF16),
    }
    for name in BLOCKS:
        n1, n2, n3 = (SIZE[a] for a in ORDER[name])
        out["gf_" + name] = pltpu.VMEM((n1, n2, n3, 16, COLS), F32)
        out["gb_" + name] = pltpu.VMEM((n1, n2, n3, 16, COLS), BF16)
        out["r0_" + name] = pltpu.VMEM((n1 - 1, n2, n3, 16, COLS), BF16)
        out["sf0_" + name] = pltpu.VMEM((n2, n3, 16, COLS), F32)
        out["sb0_" + name] = pltpu.VMEM((n2, n3, 16, COLS), BF16)
        out["r1_" + name] = pltpu.VMEM((n2 - 1, n3, 16, COLS), BF16)
        out["sf1_" + name] = pltpu.VMEM((n3, 16, COLS), F32)
        out["sb1_" + name] = pltpu.VMEM((n3, 16, COLS), BF16)
        out["r2_" + name] = pltpu.VMEM((n3 - 1, 16, COLS), BF16)
    return out


INPUTS = (
    "residuals",
    "stream",
    "token_slot",
    "level_embed",
    "embed_weight",
    "norm_gain",
    "qkv_weight",
    "out_weight",
    "out_grad",
    "teacher_map",
    "scale_table",
    "scale_row",
)
OUTPUTS = ("block_out", "qkv_weight_grad", "out_weight_grad")


def per_device(*args):
    ins = dict(zip(INPUTS, args))
    table, row = scale_tables()
    ins["norm_gain"] = ins["norm_gain"].reshape(1, D)
    ins["teacher_map"] = jnp.asarray(teacher_matrix())
    ins["scale_table"] = jnp.asarray(table, BF16)
    ins["scale_row"] = jnp.asarray(row, BF16)
    buffers = scratch()
    vmem = pl.BlockSpec(memory_space=pltpu.VMEM)
    far = pl.BlockSpec(memory_space=pl.ANY)
    return pl.pallas_call(
        functools.partial(kernel, INPUTS + OUTPUTS + tuple(buffers)),
        out_shape=(
            jax.ShapeDtypeStruct((1, SLOT, D), BF16),
            jax.ShapeDtypeStruct((16, 3, COLS), F32),
            jax.ShapeDtypeStruct((16, COLS), F32),
        ),
        in_specs=[far if n in ("qkv_weight", "out_weight") else vmem for n in INPUTS],
        out_specs=(vmem, vmem, vmem),
        scratch_shapes=list(buffers.values()),
        compiler_params=pltpu.CompilerParams(
            collective_id=0, has_side_effects=True, vmem_limit_bytes=56 << 20
        ),
    )(*[ins[n] for n in INPUTS])


def solution(mesh):
    in_specs = (
        P("img", "tok", None),
        P("img", "tok", None),
        P("img", None),
        P(),
        P(),
        P(),
        P(),
        P(),
        P("img", "tok", None),
    )
    out_specs = (P("img", "tok", None), P("img", None, "tok"), P("img", "tok"))
    return jax.shard_map(
        per_device, mesh=mesh, in_specs=in_specs, out_specs=out_specs, check_vma=False
    )
```

time: 548 us -> 61.2 us (0.11)
  waiting for transfers between devices: 372 us -> 0 us
  local copies, waits for them, and re-layouts: 67.3 us -> 4.47 us
  Pallas kernels: 0 us -> 55.8 us
  matrix products: 43.6 us -> 0 us
  starting transfers between devices: 16.7 us -> 0 us
  blocking collectives: 15.6 us -> 0 us
  other arithmetic: 14.9 us -> 0 us
  between operations: 14.8 us -> 0.64 us
    reduce_scatter x1 -> x0, waiting for transfers between devices: 319 us -> none  [per_device(): lax.psum_scatter(weight_terms(normed_all, upstream_all, query_cols[:, :,...]
    pallas_call x0 -> x1, Pallas kernels: none -> 55.8 us  [per_device(): pl.pallas_call(functools.partial(kernel, INPUTS + OUTPUTS + tuple(buffers...]
    all_gather x5 -> x0, waiting for transfers between devices: 48.9 us -> none  [the longest x1 28.7 us: per_device(): pair_all = lax.all_gather(pair_local, 'tok', axis=1, tiled=True)]
    dot_general x35 -> x0, matrix products: 41.9 us -> none  [the longest x8 7.67 us: teacher_maps(): jnp.einsum('ia,...ab,jb->...ij', upward, block_map, upward, precision=lax...]
    unnamed x70 -> x2, local copies, waits for them, and re-layouts: 24 us -> 3 us
    all_to_all x4 -> x0, starting transfers between devices: 16.3 us -> none  [the longest x1 4.74 us: per_device(): lax.all_to_all(pair_grad.astype(jnp.bfloat16), 'tok', split_axis=3, conca...]
    all_gather x2 -> x0, blocking collectives: 15.6 us -> none  [the longest x1 8.73 us: per_device(): lax.all_gather(log_total, 'tok', axis=2, tiled=True)]
    unnamed x3 -> x0, other arithmetic: 10.5 us -> none
  transfers between devices with their start and end apart: 10 -> 0, of which waited for: 5 -> 0; matrix products, arithmetic and copies ran while one was open for 15% -> 0% of each run, Pallas kernels for 0% -> 0%
where the time goes in v1:
time: 61.2 us; the launch traced here: 61 us
  Pallas kernels  55.8 us (91%)
  local copies, waits for them, and re-layouts  4.47 us (7%)
  between operations  0.64 us (1%)
    pallas_call x1, Pallas kernels, per_device(): pl.pallas_call(functools.partial(kernel, INPUTS + OUTPUTS + tuple(buffers...  55.8 us
    unnamed x2, local copies, waits for them, and re-layouts  3 us
    pallas_call x1, local copies, waits for them, and re-layouts, per_device(): pl.pallas_call(functools.partial(kernel, INPUTS + OUTPUTS + tuple(buffers...  1.47 us

profile of v1, /device:TPU:2, one launch (start us, length us, event | category | flops | bytes accessed | tf_op | source)
XLA Modules:
  0.0 61.0 jit_solution(13136486497039797764)
XLA Ops:
  0.6 55.8 %shard_map.139 = (bf16[1,136,1024]{2,1,0:T(8,128)(2,1)}, f32[16,3,256]{2,1,0:T(4,128)}, f32[16,256]{1,0:T(8,128)}) custom-call(f32[1,8,265]{2,1,0:T(8,128)} %refs_0_.1, bf16[1,136,1024]{2,1,0:T(8,128)(2,1)} %refs_1_.1, s32[1,521]{1,0:T(1,128)} %refs_2_.1, bf16[7,1024]{1,0:T(8,128)(2,1)} %refs_3_.1, bf16[32,1024]{1,0:T(8,128)(2,1)} %refs_4_.1, ...), custom_call_target="tpu_custom_call" | custom-call | tf_op jit(solution)/shard_map/pallas_call | solution.py:390
  56.5 1.5 %copy.15 = f32[16,3,256]{2,0,1:T(8,128)} copy(f32[16,3,256]{2,1,0:T(4,128)} %get-tuple-element.4) | data formatting | bytes 98304 | tf_op jit(solution)/shard_map/pallas_call | solution.py:390
  58.0 1.7 %copy.18 = bf16[1,136,1024]{2,1,0:T(8,128)(2,1)} copy(bf16[1,136,1024]{2,1,0:T(8,128)(2,1)} %get-tuple-element.9) | data formatting | bytes 557056
  59.6 1.3 %copy.19 = f32[16,256]{1,0:T(8,128)} copy(f32[16,256]{1,0:T(8,128)} %get-tuple-element.11) | data formatting | bytes 32768

commit v2 on v1

--- a/solution.py
+++ b/solution.py
@@ -21,9 +21,44 @@
 TOK_IMG = 521
 TOK_IN = 265
 SIZE = {"x": 2, "y": 4, "z": 8}
-BLOCKS = ("out", "v", "q", "k")
-ORDER = {"out": "yxz", "v": "xyz", "q": "yxz", "k": "xyz"}
-PLACE = {"q": 0, "k": 1, "v": 2}
+ORDER = {
+    ("out", 0): "zxy",
+    ("out", 1): "yxz",
+    ("v", 0): "xyz",
+    ("v", 1): "yxz",
+    ("q", 0): "xyz",
+    ("k", 0): "xyz",
+    ("q", 1): "zxy",
+    ("k", 1): "yxz",
+}
+FINISH = (
+    (("out", 1), 0),
+    (("v", 0), 0),
+    (("v", 1), 0),
+    (("q", 0), 0),
+    (("out", 0), 0),
+    (("k", 1), 0),
+    (("k", 0), 0),
+    (("out", 1), 1),
+    (("v", 0), 1),
+    (("v", 1), 1),
+    (("out", 0), 1),
+    (("q", 0), 1),
+    (("k", 1), 1),
+    (("q", 1), 0),
+    (("k", 0), 1),
+    (("out", 0), 2),
+    (("q", 1), 1),
+    (("out", 1), 2),
+    (("v", 0), 2),
+    (("v", 1), 2),
+    (("q", 0), 2),
+    (("k", 1), 2),
+    (("q", 1), 2),
+    (("k", 0), 2),
+)
+PLACE = {"q": 0, "k": 1, "v": 2, "out": 3}
+LOADED = ("residuals", "token_slot", "norm_gain", "embed_weight", "teacher_map")
 MESH = pl.DeviceIdType.MESH
 F32 = jnp.float32
 BF16 = jnp.bfloat16
@@ -57,14 +92,12 @@
     return whole.astype(np.float32)
 
 
-def scale_tables():
-    scale = np.repeat(np.arange(NSCALE), [s * s for s in SIDES])
-    table = np.zeros((TOK_IMG, 8), np.float32)
-    table[np.arange(TOK_IMG), scale] = 1.0
-    table[:, 7] = scale - NSCALE
-    row = np.zeros((8, TOK_IMG), np.float32)
-    row[0] = scale - NSCALE
-    return table, row
+def scale_of(shape, dim):
+    token = lax.broadcasted_iota(jnp.int32, shape, dim)
+    scale = jnp.full(shape, -NSCALE, jnp.int32)
+    for start in np.cumsum([side * side for side in SIDES[:-1]]):
+        scale = scale + jnp.where(token >= int(start), 1, 0)
+    return scale
 
 
 def dot(a, b, ca=1, cb=0, **kw):
@@ -117,7 +150,11 @@
                 r["qkv_weight"].at[:, pl.ds(at, COLS)], r["wq"].at[b], r["local"].at[4 + b]
             )
         )
-    for load in loads:
+    small = [
+        pltpu.make_async_copy(r[n], r["l_" + n], r["local"].at[7 + k])
+        for k, n in enumerate(LOADED)
+    ]
+    for load in small + loads:
         load.start()
 
     friends = peer[1:] + [along(a, d) for a in "xyz" for d in range(1, SIZE[a])]
@@ -126,9 +163,11 @@
         pl.semaphore_signal(barrier, inc=1, device_id=f, device_id_type=MESH)
 
     none = jnp.zeros((PAD - SLOT, D), F32)
-    r["res"][t] = r["residuals"][0]
     r["sbuf"][0] = jnp.concatenate([r["stream"][0].astype(F32), none], 0).astype(BF16)
     r["ubuf"][0] = jnp.concatenate([r["out_grad"][0].astype(F32), none], 0).astype(BF16)
+    for load in small:
+        load.wait()
+    r["res"][t] = r["l_residuals"][0]
     pl.semaphore_wait(barrier, len(friends))
 
     res_copies = [remote(r["res"].at[t], r["res"].at[t], peer[s]) for s in (1, 2, 3)]
@@ -150,15 +189,20 @@
     for s in range(SLABS):
         inside = (row >= s * PAD) & (row < s * PAD + SLOT)
         slot = jnp.where(inside, row + (tok_of[s] * SLOT - s * PAD), slot)
-    pick = jnp.where(slot == r["token_slot"][...], 1.0, 0.0).astype(BF16)
-    levels = dot(pick, r["scale_table"][...])
+    pick = jnp.where(slot == r["l_token_slot"][...], 1.0, 0.0).astype(BF16)
+    lane = lax.broadcasted_iota(jnp.int32, (TOK_IMG, 8), 1)
+    scale = scale_of((TOK_IMG, 8), 0)
+    table = jnp.where(lane == scale + NSCALE, 1, 0) + jnp.where(lane == 7, scale, 0)
+    levels = dot(pick, table.astype(F32).astype(BF16))
     sc_col = levels[:, 7:8]
     r["sc_col"][...] = sc_col
-    r["sc_row"][...] = dot(r["scale_row"][...], pick, 1, 1)
+    r["sc_row"][...] = dot(
+        scale_of((8, TOK_IMG), 1).astype(F32).astype(BF16), pick, 1, 1
+    )
     for c in res_copies:
         c.wait_recv()
     teacher = dot(
-        r["teacher_map"][...],
+        r["l_teacher_map"][...],
         r["res"][...].reshape(32, TOK_IN),
         1,
         1,
@@ -169,7 +213,7 @@
 
     def enter(s):
         at = pl.ds(s * PAD, PAD)
-        base = dot(r["chan"][at, :], r["embed_weight"][...]) + dot(
+        base = dot(r["chan"][at, :], r["l_embed_weight"][...]) + dot(
             r["lev"][at, :], r["level_embed"][...]
         )
         block_in = (base + r["sbuf"][s].astype(F32)).astype(BF16)
@@ -177,7 +221,7 @@
             r["block_in"][...] = block_in
         x = block_in.astype(F32)
         scale = lax.rsqrt(jnp.mean(x * x, axis=-1, keepdims=True) + 1e-6)
-        r["normed"][at, :] = (x * scale * r["norm_gain"][...]).astype(BF16)
+        r["normed"][at, :] = (x * scale * r["l_norm_gain"][...]).astype(BF16)
 
     def project(first):
         at = pl.ds(first * PAD, 2 * PAD)
@@ -200,6 +244,7 @@
         c.wait_recv()
     enter(3)
     project(2)
+    r["normed_t"][...] = r["normed"][...].T
 
     factor = HEAD_DIM ** (-0.5)
     heads = [slice(h * HEAD_DIM, (h + 1) * HEAD_DIM) for h in range(2)]
@@ -217,13 +262,12 @@
             r["probs"][h, at, :] = probs
             r["att"][s, :, heads[h]] = dot(probs, v).astype(BF16)
 
+    for c in range(len(pieces)):
+        u_cross[c].wait_recv()
+        u_onward[c].start()
     a_copies = [remote(r["att"].at[s], r["attin"].at[s - 1], peer[s]) for s in (1, 2, 3)]
     for c in a_copies:
         c.start()
-
-    for c in range(len(pieces)):
-        u_cross[c].wait_recv()
-        u_onward[c].start()
     u_near.wait_recv()
     for c in u_onward:
         c.wait_recv()
@@ -234,17 +278,17 @@
 
     sums = {}
 
-    def first_stage(name, rows_ref, cols):
-        order = ORDER[name]
-        g = dot(r[rows_ref][...], cols, 0, 0)
-        gf, gb = r["gf_" + name], r["gb_" + name]
-        for x in range(2):
-            for y in range(4):
-                part = g[x * 512 + y * 128 : x * 512 + (y + 1) * 128].reshape(8, 16, COLS)
-                at = tuple({"x": x, "y": y}[a] for a in order[:2])
-                gf[at] = part
-                gb[at] = part.astype(BF16)
-        return start(name, 0, gb)
+    def first_stage(names, g):
+        for n, name in enumerate(names):
+            order, gf, gb = ORDER[name], r["gf", name], r["gb", name]
+            for x in range(2):
+                for y in range(4):
+                    rows = slice(x * 512 + y * 128, x * 512 + (y + 1) * 128)
+                    part = g[rows, heads[n]].reshape(8, 16, HEAD_DIM)
+                    at = tuple({"x": x, "y": y, "z": slice(None)}[a] for a in order)
+                    gf[at] = part
+                    gb[at] = part.astype(BF16)
+            start(name, 0, gb)
 
     def start(name, stage, src):
         axis = ORDER[name][stage]
@@ -252,7 +296,7 @@
         copies = [
             remote(
                 src.at[lax.rem(mine[axis] + d, n)],
-                r[f"r{stage}_{name}"].at[d - 1],
+                r["in", stage, name].at[d - 1],
                 along(axis, d),
             )
             for d in range(1, n)
@@ -263,27 +307,25 @@
 
     def finish(name, stage):
         axis = ORDER[name][stage]
-        own = r["gf_" + name] if stage == 0 else r[f"sf{stage - 1}_{name}"]
+        own = r["gf", name] if stage == 0 else r["sf", stage - 1, name]
         for c in sums[name, stage]:
             c.wait_recv()
         total = own[mine[axis]]
         for d in range(1, SIZE[axis]):
-            total = total + r[f"r{stage}_{name}"][d - 1].astype(F32)
+            total = total + r["in", stage, name][d - 1].astype(F32)
         if stage < 2:
-            r[f"sf{stage}_{name}"][...] = total
-            r[f"sb{stage}_{name}"][...] = total.astype(BF16)
-            start(name, stage + 1, r[f"sb{stage}_{name}"])
-        elif name == "out":
-            r["out_weight_grad"][...] = total
+            r["sf", stage, name][...] = total
+            r["sb", stage, name][...] = total.astype(BF16)
+            start(name, stage + 1, r["sb", stage, name])
         else:
-            r["qkv_weight_grad"][:, PLACE[name], :] = total
+            r["weight_grad"][PLACE[name[0]], :, heads[name[1]]] = total
 
     att = jnp.concatenate([r["att"][s] for s in range(SLABS)], 0)
-    first_stage("out", "up", att)
+    first_stage((("out", 0), ("out", 1)), dot(r["up"][...], att, 0, 0))
     r["ag"][...] = dot(r["up"][...], r["ow"][0]).astype(BF16)
     for h in range(2):
         r["dv"][:, heads[h]] = dot(r["probs"][h], r["ag"][:, heads[h]], 0, 0).astype(BF16)
-    first_stage("v", "normed", r["dv"][...])
+    first_stage((("v", 0), ("v", 1)), dot(r["normed_t"][...], r["dv"][...]))
     for h in range(2):
         k, v = r["qkv"][1, :, heads[h]], r["qkv"][2, :, heads[h]]
         for s in range(SLABS):
@@ -293,12 +335,9 @@
             delta = jnp.sum(probs * dprobs, axis=-1, keepdims=True)
             ds = (probs * (dprobs - delta) * factor).astype(BF16)
             r["ds"][h, at, :] = ds
-            r["dq"][at, heads[h]] = dot(ds, k).astype(BF16)
-    first_stage("q", "normed", r["dq"][...])
-    for h in range(2):
-        r["dk"][:, heads[h]] = dot(r["ds"][h], r["qkv"][0, :, heads[h]], 0, 0).astype(BF16)
-    first_stage("k", "normed", r["dk"][...])
-    finish("out", 0)
+            r["dqk"][at, heads[0]] = dot(ds, k).astype(BF16)
+        r["dqk"][:, heads[1]] = dot(r["ds"][h], r["qkv"][0, :, heads[h]], 0, 0).astype(BF16)
+        first_stage((("q", h), ("k", h)), dot(r["normed_t"][...], r["dqk"][...]))
 
     mixed = r["block_in"][...].astype(F32) + dot(r["att"][0], r["ow"][0], 1, 1)
     for s in (1, 2, 3):
@@ -307,11 +346,8 @@
     mixed = jnp.where(r["sc_col"][pl.ds(0, PAD), :] < 0.0, mixed, 0.0)
     r["block_out"][0] = mixed[:SLOT].astype(BF16)
 
-    for name in BLOCKS[1:]:
-        finish(name, 0)
-    for stage in (1, 2):
-        for name in BLOCKS:
-            finish(name, stage)
+    for name, stage in FINISH:
+        finish(name, stage)
     for c in res_copies + s_cross + s_onward + u_cross + u_onward + a_copies + [s_near, u_near]:
         c.wait_send()
     for copies in sums.values():
@@ -321,9 +357,9 @@
 
 def scratch():
     out = {
-        "send": pltpu.SemaphoreType.DMA((68,)),
-        "recv": pltpu.SemaphoreType.DMA((68,)),
-        "local": pltpu.SemaphoreType.DMA((7,)),
+        "send": pltpu.SemaphoreType.DMA((112,)),
+        "recv": pltpu.SemaphoreType.DMA((112,)),
+        "local": pltpu.SemaphoreType.DMA((7 + len(LOADED),)),
         "ow": pltpu.VMEM((SLABS, D, COLS), BF16),
         "wq": pltpu.VMEM((3, D, COLS), BF16),
         "res": pltpu.VMEM((4, 8, TOK_IN), F32),
@@ -343,21 +379,33 @@
         "attin": pltpu.VMEM((SLABS - 1, PAD, COLS), BF16),
         "ag": pltpu.VMEM((ROWS, COLS), BF16),
         "dv": pltpu.VMEM((ROWS, COLS), BF16),
-        "dq": pltpu.VMEM((ROWS, COLS), BF16),
-        "dk": pltpu.VMEM((ROWS, COLS), BF16),
+        "dqk": pltpu.VMEM((ROWS, COLS), BF16),
+        "normed_t": pltpu.VMEM((D, ROWS), BF16),
+        "l_residuals": pltpu.VMEM((1, 8, TOK_IN), F32),
+        "l_token_slot": pltpu.VMEM((1, TOK_IMG), jnp.int32),
+        "l_norm_gain": pltpu.VMEM((1, D), F32),
+        "l_embed_weight": pltpu.VMEM((32, D), BF16),
+        "l_teacher_map": pltpu.VMEM((TOK_IMG, TOK_IN), F32),
     }
-    for name in BLOCKS:
-        n1, n2, n3 = (SIZE[a] for a in ORDER[name])
-        out["gf_" + name] = pltpu.VMEM((n1, n2, n3, 16, COLS), F32)
-        out["gb_" + name] = pltpu.VMEM((n1, n2, n3, 16, COLS), BF16)
-        out["r0_" + name] = pltpu.VMEM((n1 - 1, n2, n3, 16, COLS), BF16)
-        out["sf0_" + name] = pltpu.VMEM((n2, n3, 16, COLS), F32)
-        out["sb0_" + name] = pltpu.VMEM((n2, n3, 16, COLS), BF16)
-        out["r1_" + name] = pltpu.VMEM((n2 - 1, n3, 16, COLS), BF16)
-        out["sf1_" + name] = pltpu.VMEM((n3, 16, COLS), F32)
-        out["sb1_" + name] = pltpu.VMEM((n3, 16, COLS), BF16)
-        out["r2_" + name] = pltpu.VMEM((n3 - 1, 16, COLS), BF16)
+    for name, order in ORDER.items():
+        n1, n2, n3 = (SIZE[a] for a in order)
+        tail = (16, HEAD_DIM)
+        out["gf", name] = pltpu.VMEM((n1, n2, n3) + tail, F32)
+        out["gb", name] = pltpu.VMEM((n1, n2, n3) + tail, BF16)
+        out["in", 0, name] = pltpu.VMEM((n1 - 1, n2, n3) + tail, BF16)
+        out["sf", 0, name] = pltpu.VMEM((n2, n3) + tail, F32)
+        out["sb", 0, name] = pltpu.VMEM((n2, n3) + tail, BF16)
+        out["in", 1, name] = pltpu.VMEM((n2 - 1, n3) + tail, BF16)
+        out["sf", 1, name] = pltpu.VMEM((n3,) + tail, F32)
+        out["sb", 1, name] = pltpu.VMEM((n3,) + tail, BF16)
+        out["in", 2, name] = pltpu.VMEM((n3 - 1,) + tail, BF16)
     return out
+
+
+def hand_over(block_in, weight_in, block_out, qkv_out, out_out):
+    block_out[...] = block_in[...]
+    qkv_out[...] = weight_in[:3]
+    out_out[...] = weight_in[3]
 
 
 INPUTS = (
@@ -371,36 +419,40 @@
     "out_weight",
     "out_grad",
     "teacher_map",
-    "scale_table",
-    "scale_row",
 )
-OUTPUTS = ("block_out", "qkv_weight_grad", "out_weight_grad")
+OUTPUTS = ("block_out", "weight_grad")
+HELD = ("stream", "out_grad", "level_embed")
 
 
 def per_device(*args):
     ins = dict(zip(INPUTS, args))
-    table, row = scale_tables()
     ins["norm_gain"] = ins["norm_gain"].reshape(1, D)
     ins["teacher_map"] = jnp.asarray(teacher_matrix())
-    ins["scale_table"] = jnp.asarray(table, BF16)
-    ins["scale_row"] = jnp.asarray(row, BF16)
     buffers = scratch()
     vmem = pl.BlockSpec(memory_space=pltpu.VMEM)
     far = pl.BlockSpec(memory_space=pl.ANY)
-    return pl.pallas_call(
+    block_shape = jax.ShapeDtypeStruct((1, SLOT, D), BF16)
+    block_out, weight_grad = pl.pallas_call(
         functools.partial(kernel, INPUTS + OUTPUTS + tuple(buffers)),
-        out_shape=(
-            jax.ShapeDtypeStruct((1, SLOT, D), BF16),
-            jax.ShapeDtypeStruct((16, 3, COLS), F32),
-            jax.ShapeDtypeStruct((16, COLS), F32),
-        ),
-        in_specs=[far if n in ("qkv_weight", "out_weight") else vmem for n in INPUTS],
-        out_specs=(vmem, vmem, vmem),
+        out_shape=(block_shape, jax.ShapeDtypeStruct((4, 16, COLS), F32)),
+        in_specs=[vmem if n in HELD else far for n in INPUTS],
+        out_specs=(vmem, vmem),
         scratch_shapes=list(buffers.values()),
         compiler_params=pltpu.CompilerParams(
             collective_id=0, has_side_effects=True, vmem_limit_bytes=56 << 20
         ),
     )(*[ins[n] for n in INPUTS])
+    block_out, qkv_grad, out_grad = pl.pallas_call(
+        hand_over,
+        out_shape=(
+            block_shape,
+            jax.ShapeDtypeStruct((3, 16, COLS), F32),
+            jax.ShapeDtypeStruct((16, COLS), F32),
+        ),
+        in_specs=[vmem] * 2,
+        out_specs=(vmem,) * 3,
+    )(block_out, weight_grad)
+    return block_out, qkv_grad.transpose(1, 0, 2), out_grad
 
 
 def solution(mesh):

time: 61.2 us -> 56.8 us (0.928)
  local copies, waits for them, and re-layouts: 4.47 us -> 0 us
    unnamed x2 -> x0, local copies, waits for them, and re-layouts: 3 us -> none
    pallas_call x0 -> x1, Pallas kernels: none -> 1.69 us  [per_device(): pl.pallas_call(hand_over, out_shape=(block_shape, jax.ShapeDtypeStruct((3...]
    pallas_call x1, Pallas kernels: 55.8 us -> 54.3 us  [per_device(): pl.pallas_call(functools.partial(kernel, INPUTS + OUTPUTS + tuple(buffers...]
    pallas_call x1 -> x0, local copies, waits for them, and re-layouts: 1.47 us -> none  [per_device(): pl.pallas_call(functools.partial(kernel, INPUTS + OUTPUTS + tuple(buffers...]
where the time goes in v2:
time: 56.8 us; the launch traced here: 56.6 us
  Pallas kernels  56 us (99%)
  between operations  0.64 us (1%)
    pallas_call x1, Pallas kernels, per_device(): pl.pallas_call(functools.partial(kernel, INPUTS + OUTPUTS + tuple(buffers...  54.3 us
    pallas_call x1, Pallas kernels, per_device(): pl.pallas_call(hand_over, out_shape=(block_shape, jax.ShapeDtypeStruct((3...  1.69 us

profile of v2, /device:TPU:2, one launch (start us, length us, event | category | flops | bytes accessed | tf_op | source)
XLA Modules:
  0.0 56.6 jit_solution(12934731676828346891)
XLA Ops:
  0.6 54.3 %shard_map.121 = (bf16[1,136,1024]{2,1,0:T(8,128)(2,1)}, f32[4,16,256]{2,1,0:T(8,128)}) custom-call(f32[1,8,265]{2,1,0:T(8,128)} %refs_0_.1, bf16[1,136,1024]{2,1,0:T(8,128)(2,1)} %refs_1_.1, s32[1,521]{1,0:T(1,128)} %refs_2_.1, bf16[7,1024]{1,0:T(8,128)(2,1)} %refs_3_.1, bf16[32,1024]{1,0:T(8,128)(2,1)} %refs_4_.1, f32[1,1024]{1,0:T(1,128)} %bitcast.2, ...), custom_call_target="tpu_custom_call" | custom-call | tf_op jit(solution)/shard_map/pallas_call | solution.py:435
  54.9 1.7 %shard_map.122 = (bf16[1,136,1024]{2,1,0:T(8,128)(2,1)}, f32[3,16,256]{2,1,0:T(8,128)}, f32[16,256]{1,0:T(8,128)}) custom-call(bf16[1,136,1024]{2,1,0:T(8,128)(2,1)} %get-tuple-element.8.block_in, f32[4,16,256]{2,1,0:T(8,128)} %get-tuple-element.9.weight_in), custom_call_target="tpu_custom_call" | custom-call | tf_op jit(solution)/shard_map/pallas_call | solution.py:445

commit v3 on v2

--- a/solution.py
+++ b/solution.py
@@ -58,7 +58,15 @@
     (("k", 0), 2),
 )
 PLACE = {"q": 0, "k": 1, "v": 2, "out": 3}
-LOADED = ("residuals", "token_slot", "norm_gain", "embed_weight", "teacher_map")
+LOADED = (
+    "stream",
+    "residuals",
+    "token_slot",
+    "norm_gain",
+    "embed_weight",
+    "teacher_map",
+    "out_grad",
+)
 MESH = pl.DeviceIdType.MESH
 F32 = jnp.float32
 BF16 = jnp.bfloat16
@@ -120,69 +128,72 @@
         at[axis] = lax.rem(mine[axis] + d, SIZE[axis])
         return ((at["x"] * 4 + at["y"]) * 8 + at["z"], t)
 
-    send, recv = r["send"], r["recv"]
-    used = [0]
-
-    def remote(src, dst, device):
-        n = used[0]
+    friends = peer[1:] + [along(a, d) for a in "xyz" for d in range(1, SIZE[a])]
+    barrier = pltpu.get_barrier_semaphore()
+    for f in friends:
+        pl.semaphore_signal(barrier, inc=1, device_id=f, device_id_type=MESH)
+
+    sems, used = r["sems"], [0]
+
+    def new_sem():
         used[0] += 1
+        return sems.at[used[0] - 1]
+
+    def remote(src, dst, device, send_sem, recv_sem):
         return pltpu.make_async_remote_copy(
             src_ref=src,
             dst_ref=dst,
-            send_sem=send.at[n],
-            recv_sem=recv.at[n],
+            send_sem=send_sem,
+            recv_sem=recv_sem,
             device_id=device,
             device_id_type=MESH,
         )
 
+    def wait_bytes(ref, sem):
+        pltpu.make_async_copy(ref, ref, sem).wait()
+
+    small = {n: pltpu.make_async_copy(r[n], r["l_" + n], new_sem()) for n in LOADED}
+    ow_sem, wq_sem = new_sem(), new_sem()
     loads = []
     for s in range(SLABS):
         at = pl.multiple_of(tok_of[s] * COLS, COLS)
         loads.append(
-            pltpu.make_async_copy(
-                r["out_weight"].at[:, pl.ds(at, COLS)], r["ow"].at[s], r["local"].at[s]
-            )
+            pltpu.make_async_copy(r["out_weight"].at[:, pl.ds(at, COLS)], r["ow"].at[s], ow_sem)
         )
     for b in range(3):
         at = pl.multiple_of(b * D + t * COLS, COLS)
         loads.append(
-            pltpu.make_async_copy(
-                r["qkv_weight"].at[:, pl.ds(at, COLS)], r["wq"].at[b], r["local"].at[4 + b]
-            )
+            pltpu.make_async_copy(r["qkv_weight"].at[:, pl.ds(at, COLS)], r["wq"].at[b], wq_sem)
         )
-    small = [
-        pltpu.make_async_copy(r[n], r["l_" + n], r["local"].at[7 + k])
-        for k, n in enumerate(LOADED)
-    ]
-    for load in small + loads:
+    for load in list(small.values()) + loads:
         load.start()
 
-    friends = peer[1:] + [along(a, d) for a in "xyz" for d in range(1, SIZE[a])]
-    barrier = pltpu.get_barrier_semaphore()
-    for f in friends:
-        pl.semaphore_signal(barrier, inc=1, device_id=f, device_id_type=MESH)
-
     none = jnp.zeros((PAD - SLOT, D), F32)
-    r["sbuf"][0] = jnp.concatenate([r["stream"][0].astype(F32), none], 0).astype(BF16)
-    r["ubuf"][0] = jnp.concatenate([r["out_grad"][0].astype(F32), none], 0).astype(BF16)
-    for load in small:
-        load.wait()
+    small["stream"].wait()
+    r["sbuf"][0] = jnp.concatenate([r["l_stream"][0].astype(F32), none], 0).astype(BF16)
+    small["residuals"].wait()
     r["res"][t] = r["l_residuals"][0]
     pl.semaphore_wait(barrier, len(friends))
 
-    res_copies = [remote(r["res"].at[t], r["res"].at[t], peer[s]) for s in (1, 2, 3)]
+    res_copies = [
+        remote(r["res"].at[t], r["res"].at[t], peer[s], new_sem(), new_sem()) for s in (1, 2, 3)
+    ]
     pieces = [pl.ds(CHUNK * c, CHUNK) for c in range(PAD // CHUNK)]
 
     def gather_copies(buf):
-        cross = [remote(buf.at[0, p], buf.at[2, p], peer[2]) for p in pieces]
-        near = remote(buf.at[0], buf.at[1], peer[1])
-        onward = [remote(buf.at[2, p], buf.at[3, p], peer[1]) for p in pieces]
-        return cross, near, onward
-
-    s_cross, s_near, s_onward = gather_copies(r["sbuf"])
-    u_cross, u_near, u_onward = gather_copies(r["ubuf"])
+        sent, onward_sem = new_sem(), new_sem()
+        cross = [remote(buf.at[0, p], buf.at[2, p], peer[2], sent, new_sem()) for p in pieces]
+        near = remote(buf.at[0], buf.at[1], peer[1], sent, new_sem())
+        onward = [remote(buf.at[2, p], buf.at[3, p], peer[1], sent, onward_sem) for p in pieces]
+        return cross, near, onward, sent, onward_sem
+
+    s_cross, s_near, s_onward, s_sent, s_onward_sem = gather_copies(r["sbuf"])
+    u_cross, u_near, u_onward, u_sent, u_onward_sem = gather_copies(r["ubuf"])
     for c in res_copies + s_cross + [s_near]:
         c.start()
+    for n in LOADED[2:]:
+        small[n].wait()
+    r["ubuf"][0] = jnp.concatenate([r["l_out_grad"][0].astype(F32), none], 0).astype(BF16)
 
     row = lax.broadcasted_iota(jnp.int32, (ROWS, 1), 0)
     slot = jnp.full((ROWS, 1), -1, jnp.int32)
@@ -231,8 +242,8 @@
     enter(0)
     s_near.wait_recv()
     enter(1)
-    for load in loads:
-        load.wait()
+    wait_bytes(r["ow"], ow_sem)
+    wait_bytes(r["wq"], wq_sem)
     project(0)
     for c in range(len(pieces)):
         s_cross[c].wait_recv()
@@ -240,8 +251,7 @@
         u_cross[c].start()
     u_near.start()
     enter(2)
-    for c in s_onward:
-        c.wait_recv()
+    wait_bytes(r["sbuf"].at[3], s_onward_sem)
     enter(3)
     project(2)
     r["normed_t"][...] = r["normed"][...].T
@@ -265,60 +275,72 @@
     for c in range(len(pieces)):
         u_cross[c].wait_recv()
         u_onward[c].start()
-    a_copies = [remote(r["att"].at[s], r["attin"].at[s - 1], peer[s]) for s in (1, 2, 3)]
-    for c in a_copies:
-        c.start()
+    a_sent, a_come = new_sem(), new_sem()
+    for s in (1, 2, 3):
+        remote(r["att"].at[s], r["attin"].at[s - 1], peer[s], a_sent, a_come).start()
     u_near.wait_recv()
-    for c in u_onward:
-        c.wait_recv()
+    wait_bytes(r["ubuf"].at[3], u_onward_sem)
     for s in range(SLABS):
         at = pl.ds(s * PAD, PAD)
         up = jnp.where(r["sc_col"][at, :] < 0.0, r["ubuf"][s].astype(F32), 0.0)
         r["up"][at, :] = up.astype(BF16)
 
-    sums = {}
+    piece_sent, arrival = {}, {}
+
+    def tiles(name, stage):
+        sizes = [SIZE[a] for a in ORDER[name]]
+        share = (64, 32, 16, 8, 4, 2, 1)[sum(n.bit_length() - 1 for n in sizes[: stage + 1])]
+        first = 64 - share * sizes[stage]
+        return sizes[stage], share, first
 
     def first_stage(names, g):
         for n, name in enumerate(names):
             order, gf, gb = ORDER[name], r["gf", name], r["gb", name]
+            _, n2, n3 = (SIZE[a] for a in order)
+            step = {order[0]: n2 * n3, order[1]: n3, order[2]: 1}
             for x in range(2):
                 for y in range(4):
                     rows = slice(x * 512 + y * 128, x * 512 + (y + 1) * 128)
                     part = g[rows, heads[n]].reshape(8, 16, HEAD_DIM)
-                    at = tuple({"x": x, "y": y, "z": slice(None)}[a] for a in order)
-                    gf[at] = part
-                    gb[at] = part.astype(BF16)
+                    at = x * step["x"] + y * step["y"]
+                    if step["z"] == 1:
+                        gf[at : at + 8] = part
+                        gb[at : at + 8] = part.astype(BF16)
+                    else:
+                        for z in range(8):
+                            gf[at + z * step["z"]] = part[z]
+                            gb[at + z * step["z"]] = part[z].astype(BF16)
+            piece_sent[name] = new_sem()
             start(name, 0, gb)
 
     def start(name, stage, src):
         axis = ORDER[name][stage]
-        n = SIZE[axis]
-        copies = [
+        n, share, first = tiles(name, stage)
+        arrival[name, stage] = new_sem()
+        for d in range(1, n):
             remote(
-                src.at[lax.rem(mine[axis] + d, n)],
-                r["in", stage, name].at[d - 1],
+                src.at[pl.ds(lax.rem(mine[axis] + d, n) * share, share)],
+                r["in", name].at[pl.ds(first + (d - 1) * share, share)],
                 along(axis, d),
-            )
-            for d in range(1, n)
-        ]
-        for c in copies:
-            c.start()
-        sums[name, stage] = copies
+                piece_sent[name],
+                arrival[name, stage],
+            ).start()
 
     def finish(name, stage):
         axis = ORDER[name][stage]
+        n, share, first = tiles(name, stage)
+        come = r["in", name]
+        wait_bytes(come.at[pl.ds(first, (n - 1) * share)], arrival[name, stage])
         own = r["gf", name] if stage == 0 else r["sf", stage - 1, name]
-        for c in sums[name, stage]:
-            c.wait_recv()
-        total = own[mine[axis]]
-        for d in range(1, SIZE[axis]):
-            total = total + r["in", stage, name][d - 1].astype(F32)
+        total = own[pl.ds(mine[axis] * share, share)]
+        for d in range(1, n):
+            total = total + come[pl.ds(first + (d - 1) * share, share)].astype(F32)
         if stage < 2:
             r["sf", stage, name][...] = total
             r["sb", stage, name][...] = total.astype(BF16)
             start(name, stage + 1, r["sb", stage, name])
         else:
-            r["weight_grad"][PLACE[name[0]], :, heads[name[1]]] = total
+            r["weight_grad"][PLACE[name[0]], :, heads[name[1]]] = total[0]
 
     att = jnp.concatenate([r["att"][s] for s in range(SLABS)], 0)
     first_stage((("out", 0), ("out", 1)), dot(r["up"][...], att, 0, 0))
@@ -339,27 +361,27 @@
         r["dqk"][:, heads[1]] = dot(r["ds"][h], r["qkv"][0, :, heads[h]], 0, 0).astype(BF16)
         first_stage((("q", h), ("k", h)), dot(r["normed_t"][...], r["dqk"][...]))
 
+    wait_bytes(r["attin"], a_come)
     mixed = r["block_in"][...].astype(F32) + dot(r["att"][0], r["ow"][0], 1, 1)
     for s in (1, 2, 3):
-        a_copies[s - 1].wait_recv()
         mixed = mixed + dot(r["attin"][s - 1], r["ow"][s], 1, 1)
     mixed = jnp.where(r["sc_col"][pl.ds(0, PAD), :] < 0.0, mixed, 0.0)
     r["block_out"][0] = mixed[:SLOT].astype(BF16)
 
     for name, stage in FINISH:
         finish(name, stage)
-    for c in res_copies + s_cross + s_onward + u_cross + u_onward + a_copies + [s_near, u_near]:
+    for c in res_copies:
         c.wait_send()
-    for copies in sums.values():
-        for c in copies:
-            c.wait_send()
+    wait_bytes(r["sbuf"].at[pl.ds(1, 3)], s_sent)
+    wait_bytes(r["ubuf"].at[pl.ds(1, 3)], u_sent)
+    wait_bytes(r["attin"], a_sent)
+    for name in ORDER:
+        wait_bytes(r["in", name], piece_sent[name])
 
 
 def scratch():
     out = {
-        "send": pltpu.SemaphoreType.DMA((112,)),
-        "recv": pltpu.SemaphoreType.DMA((112,)),
-        "local": pltpu.SemaphoreType.DMA((7 + len(LOADED),)),
+        "sems": pltpu.SemaphoreType.DMA((len(LOADED) + 2 + 6 + 12 + 2 + 32,)),
         "ow": pltpu.VMEM((SLABS, D, COLS), BF16),
         "wq": pltpu.VMEM((3, D, COLS), BF16),
         "res": pltpu.VMEM((4, 8, TOK_IN), F32),
@@ -381,6 +403,8 @@
         "dv": pltpu.VMEM((ROWS, COLS), BF16),
         "dqk": pltpu.VMEM((ROWS, COLS), BF16),
         "normed_t": pltpu.VMEM((D, ROWS), BF16),
+        "l_stream": pltpu.VMEM((1, SLOT, D), BF16),
+        "l_out_grad": pltpu.VMEM((1, SLOT, D), BF16),
         "l_residuals": pltpu.VMEM((1, 8, TOK_IN), F32),
         "l_token_slot": pltpu.VMEM((1, TOK_IMG), jnp.int32),
         "l_norm_gain": pltpu.VMEM((1, D), F32),
@@ -388,17 +412,14 @@
         "l_teacher_map": pltpu.VMEM((TOK_IMG, TOK_IN), F32),
     }
     for name, order in ORDER.items():
-        n1, n2, n3 = (SIZE[a] for a in order)
+        _, n2, n3 = (SIZE[a] for a in order)
         tail = (16, HEAD_DIM)
-        out["gf", name] = pltpu.VMEM((n1, n2, n3) + tail, F32)
-        out["gb", name] = pltpu.VMEM((n1, n2, n3) + tail, BF16)
-        out["in", 0, name] = pltpu.VMEM((n1 - 1, n2, n3) + tail, BF16)
-        out["sf", 0, name] = pltpu.VMEM((n2, n3) + tail, F32)
-        out["sb", 0, name] = pltpu.VMEM((n2, n3) + tail, BF16)
-        out["in", 1, name] = pltpu.VMEM((n2 - 1, n3) + tail, BF16)
-        out["sf", 1, name] = pltpu.VMEM((n3,) + tail, F32)
-        out["sb", 1, name] = pltpu.VMEM((n3,) + tail, BF16)
-        out["in", 2, name] = pltpu.VMEM((n3 - 1,) + tail, BF16)
+        out["gf", name] = pltpu.VMEM((64,) + tail, F32)
+        out["gb", name] = pltpu.VMEM((64,) + tail, BF16)
+        out["in", name] = pltpu.VMEM((63,) + tail, BF16)
+        for stage, share in ((0, n2 * n3), (1, n3)):
+            out["sf", stage, name] = pltpu.VMEM((share,) + tail, F32)
+            out["sb", stage, name] = pltpu.VMEM((share,) + tail, BF16)
     return out
 
 
@@ -421,7 +442,7 @@
     "teacher_map",
 )
 OUTPUTS = ("block_out", "weight_grad")
-HELD = ("stream", "out_grad", "level_embed")
+HELD = ("level_embed",)
 
 
 def per_device(*args):

time: 56.8 us -> 54.5 us (0.960)
  Pallas kernels: 56 us -> 53.7 us
    pallas_call x1, Pallas kernels: 54.3 us -> 52 us  [per_device(): pl.pallas_call(functools.partial(kernel, INPUTS + OUTPUTS + tuple(buffers...]
where the time goes in v3:
time: 54.5 us; the launch traced here: 54.3 us
  Pallas kernels  53.7 us (99%)
  between operations  0.64 us (1%)
    pallas_call x1, Pallas kernels, per_device(): pl.pallas_call(functools.partial(kernel, INPUTS + OUTPUTS + tuple(buffers...  52 us
    pallas_call x1, Pallas kernels, per_device(): pl.pallas_call(hand_over, out_shape=(block_shape, jax.ShapeDtypeStruct((3...  1.69 us

profile of v3, /device:TPU:2, one launch (start us, length us, event | category | flops | bytes accessed | tf_op | source)
XLA Modules:
  0.0 54.3 jit_solution(12019516442039470051)
XLA Ops:
  0.6 52.0 %shard_map.121 = (bf16[1,136,1024]{2,1,0:T(8,128)(2,1)}, f32[4,16,256]{2,1,0:T(8,128)}) custom-call(f32[1,8,265]{2,1,0:T(8,128)} %refs_0_.1, bf16[1,136,1024]{2,1,0:T(8,128)(2,1)} %refs_1_.1, s32[1,521]{1,0:T(1,128)} %refs_2_.1, bf16[7,1024]{1,0:T(8,128)(2,1)} %refs_3_.1, bf16[32,1024]{1,0:T(8,128)(2,1)} %refs_4_.1, f32[1,1024]{1,0:T(1,128)} %bitcast.2, ...), custom_call_target="tpu_custom_call" | custom-call | tf_op jit(solution)/shard_map/pallas_call | solution.py:456
  52.6 1.7 %shard_map.122 = (bf16[1,136,1024]{2,1,0:T(8,128)(2,1)}, f32[3,16,256]{2,1,0:T(8,128)}, f32[16,256]{1,0:T(8,128)}) custom-call(bf16[1,136,1024]{2,1,0:T(8,128)(2,1)} %get-tuple-element.8.block_in, f32[4,16,256]{2,1,0:T(8,128)} %get-tuple-element.9.weight_in), custom_call_target="tpu_custom_call" | custom-call | tf_op jit(solution)/shard_map/pallas_call | solution.py:466

commit v4 on v3

--- a/solution.py
+++ b/solution.py
@@ -23,39 +23,39 @@
 SIZE = {"x": 2, "y": 4, "z": 8}
 ORDER = {
     ("out", 0): "zxy",
-    ("out", 1): "yxz",
+    ("out", 1): "yzx",
     ("v", 0): "xyz",
     ("v", 1): "yxz",
-    ("q", 0): "xyz",
+    ("q", 0): "zxy",
     ("k", 0): "xyz",
-    ("q", 1): "zxy",
+    ("q", 1): "xyz",
     ("k", 1): "yxz",
 }
 FINISH = (
     (("out", 1), 0),
     (("v", 0), 0),
     (("v", 1), 0),
-    (("q", 0), 0),
+    (("k", 0), 0),
     (("out", 0), 0),
     (("k", 1), 0),
-    (("k", 0), 0),
+    (("q", 1), 0),
+    (("v", 1), 1),
+    (("v", 0), 1),
+    (("out", 0), 1),
+    (("k", 0), 1),
+    (("k", 1), 1),
+    (("q", 0), 0),
+    (("q", 1), 1),
+    (("out", 0), 2),
     (("out", 1), 1),
-    (("v", 0), 1),
-    (("v", 1), 1),
-    (("out", 0), 1),
+    (("v", 1), 2),
     (("q", 0), 1),
-    (("k", 1), 1),
-    (("q", 1), 0),
-    (("k", 0), 1),
-    (("out", 0), 2),
-    (("q", 1), 1),
+    (("v", 0), 2),
     (("out", 1), 2),
-    (("v", 0), 2),
-    (("v", 1), 2),
+    (("k", 0), 2),
+    (("k", 1), 2),
     (("q", 0), 2),
-    (("k", 1), 2),
     (("q", 1), 2),
-    (("k", 0), 2),
 )
 PLACE = {"q": 0, "k": 1, "v": 2, "out": 3}
 LOADED = (
@@ -64,6 +64,7 @@
     "token_slot",
     "norm_gain",
     "embed_weight",
+    "level_embed",
     "teacher_map",
     "out_grad",
 )
@@ -182,7 +183,7 @@
 
     def gather_copies(buf):
         sent, onward_sem = new_sem(), new_sem()
-        cross = [remote(buf.at[0, p], buf.at[2, p], peer[2], sent, new_sem()) for p in pieces]
+        cross = [remote(buf.at[0, p], buf.at[2, p], peer[2], new_sem(), new_sem()) for p in pieces]
         near = remote(buf.at[0], buf.at[1], peer[1], sent, new_sem())
         onward = [remote(buf.at[2, p], buf.at[3, p], peer[1], sent, onward_sem) for p in pieces]
         return cross, near, onward, sent, onward_sem
@@ -225,7 +226,7 @@
     def enter(s):
         at = pl.ds(s * PAD, PAD)
         base = dot(r["chan"][at, :], r["l_embed_weight"][...]) + dot(
-            r["lev"][at, :], r["level_embed"][...]
+            r["lev"][at, :], r["l_level_embed"][...]
         )
         block_in = (base + r["sbuf"][s].astype(F32)).astype(BF16)
         if s == 0:
@@ -246,15 +247,16 @@
     wait_bytes(r["wq"], wq_sem)
     project(0)
     for c in range(len(pieces)):
+        s_cross[c].wait_send()
+        u_cross[c].start()
+    for c in range(len(pieces)):
         s_cross[c].wait_recv()
         s_onward[c].start()
-        u_cross[c].start()
     u_near.start()
     enter(2)
     wait_bytes(r["sbuf"].at[3], s_onward_sem)
     enter(3)
     project(2)
-    r["normed_t"][...] = r["normed"][...].T
 
     factor = HEAD_DIM ** (-0.5)
     heads = [slice(h * HEAD_DIM, (h + 1) * HEAD_DIM) for h in range(2)]
@@ -262,11 +264,11 @@
         k, v = r["qkv"][1, :, heads[h]], r["qkv"][2, :, heads[h]]
         for s in range(SLABS):
             at = pl.ds(s * PAD, PAD)
-            scores = dot(r["qkv"][0, at, heads[h]], k, 1, 1) * factor
+            scores = dot(r["qkv"][0, at, heads[h]], k, 1, 1)
             allowed = r["sc_row"][0:1, :] <= r["sc_col"][at, :]
             scores = jnp.where(allowed, scores, -jnp.inf)
             top = jnp.max(scores, axis=-1, keepdims=True)
-            expd = jnp.exp(scores - top)
+            expd = jnp.exp2((scores - top) * (factor * np.log2(np.e)))
             total = jnp.sum(expd, axis=-1, keepdims=True)
             probs = (expd * (1.0 / total)).astype(BF16)
             r["probs"][h, at, :] = probs
@@ -344,6 +346,7 @@
 
     att = jnp.concatenate([r["att"][s] for s in range(SLABS)], 0)
     first_stage((("out", 0), ("out", 1)), dot(r["up"][...], att, 0, 0))
+    r["normed_t"][...] = r["normed"][...].T
     r["ag"][...] = dot(r["up"][...], r["ow"][0]).astype(BF16)
     for h in range(2):
         r["dv"][:, heads[h]] = dot(r["probs"][h], r["ag"][:, heads[h]], 0, 0).astype(BF16)
@@ -366,14 +369,19 @@
     for s in (1, 2, 3):
         mixed = mixed + dot(r["attin"][s - 1], r["ow"][s], 1, 1)
     mixed = jnp.where(r["sc_col"][pl.ds(0, PAD), :] < 0.0, mixed, 0.0)
-    r["block_out"][0] = mixed[:SLOT].astype(BF16)
+    r["done"][0] = mixed[:SLOT].astype(BF16)
+    block_write = pltpu.make_async_copy(r["done"], r["block_out"], new_sem())
+    block_write.start()
 
     for name, stage in FINISH:
         finish(name, stage)
+    block_write.wait()
     for c in res_copies:
         c.wait_send()
-    wait_bytes(r["sbuf"].at[pl.ds(1, 3)], s_sent)
-    wait_bytes(r["ubuf"].at[pl.ds(1, 3)], u_sent)
+    for c in u_cross:
+        c.wait_send()
+    wait_bytes(r["sbuf"].at[pl.ds(1, 2)], s_sent)
+    wait_bytes(r["ubuf"].at[pl.ds(1, 2)], u_sent)
     wait_bytes(r["attin"], a_sent)
     for name in ORDER:
         wait_bytes(r["in", name], piece_sent[name])
@@ -381,7 +389,7 @@
 
 def scratch():
     out = {
-        "sems": pltpu.SemaphoreType.DMA((len(LOADED) + 2 + 6 + 12 + 2 + 32,)),
+        "sems": pltpu.SemaphoreType.DMA((len(LOADED) + 2 + 6 + 18 + 2 + 33,)),
         "ow": pltpu.VMEM((SLABS, D, COLS), BF16),
         "wq": pltpu.VMEM((3, D, COLS), BF16),
         "res": pltpu.VMEM((4, 8, TOK_IN), F32),
@@ -405,9 +413,11 @@
         "normed_t": pltpu.VMEM((D, ROWS), BF16),
         "l_stream": pltpu.VMEM((1, SLOT, D), BF16),
         "l_out_grad": pltpu.VMEM((1, SLOT, D), BF16),
+        "done": pltpu.VMEM((1, SLOT, D), BF16),
         "l_residuals": pltpu.VMEM((1, 8, TOK_IN), F32),
         "l_token_slot": pltpu.VMEM((1, TOK_IMG), jnp.int32),
         "l_norm_gain": pltpu.VMEM((1, D), F32),
+        "l_level_embed": pltpu.VMEM((NSCALE, D), BF16),
         "l_embed_weight": pltpu.VMEM((32, D), BF16),
         "l_teacher_map": pltpu.VMEM((TOK_IMG, TOK_IN), F32),
     }
@@ -442,7 +452,6 @@
     "teacher_map",
 )
 OUTPUTS = ("block_out", "weight_grad")
-HELD = ("level_embed",)
 
 
 def per_device(*args):
@@ -456,8 +465,8 @@
     block_out, weight_grad = pl.pallas_call(
         functools.partial(kernel, INPUTS + OUTPUTS + tuple(buffers)),
         out_shape=(block_shape, jax.ShapeDtypeStruct((4, 16, COLS), F32)),
-        in_specs=[vmem if n in HELD else far for n in INPUTS],
-        out_specs=(vmem, vmem),
+        in_specs=[far] * len(INPUTS),
+        out_specs=(far, vmem),
         scratch_shapes=list(buffers.values()),
         compiler_params=pltpu.CompilerParams(
             collective_id=0, has_side_effects=True, vmem_limit_bytes=56 << 20

time: 54.5 us -> 53.8 us (0.987)
  Pallas kernels: 53.7 us -> 53.1 us
    pallas_call x1, Pallas kernels: 52 us -> 51.4 us  [per_device(): pl.pallas_call(functools.partial(kernel, INPUTS + OUTPUTS + tuple(buffers...]
where the time goes in v4:
time: 53.8 us; the launch traced here: 53.7 us
  Pallas kernels  53.1 us (99%)
  between operations  0.64 us (1%)
    pallas_call x1, Pallas kernels, per_device(): pl.pallas_call(functools.partial(kernel, INPUTS + OUTPUTS + tuple(buffers...  51.4 us
    pallas_call x1, Pallas kernels, per_device(): pl.pallas_call(hand_over, out_shape=(block_shape, jax.ShapeDtypeStruct((3...  1.69 us

profile of v4, /device:TPU:2, one launch (start us, length us, event | category | flops | bytes accessed | tf_op | source)
XLA Modules:
  0.0 53.7 jit_solution(6308269650589948090)
XLA Ops:
  0.6 51.4 %shard_map.121 = (bf16[1,136,1024]{2,1,0:T(8,128)(2,1)}, f32[4,16,256]{2,1,0:T(8,128)}) custom-call(f32[1,8,265]{2,1,0:T(8,128)} %refs_0_.1, bf16[1,136,1024]{2,1,0:T(8,128)(2,1)} %refs_1_.1, s32[1,521]{1,0:T(1,128)} %refs_2_.1, bf16[7,1024]{1,0:T(8,128)(2,1)} %refs_3_.1, bf16[32,1024]{1,0:T(8,128)(2,1)} %refs_4_.1, f32[1,1024]{1,0:T(1,128)} %bitcast.2, ...), custom_call_target="tpu_custom_call" | custom-call | tf_op jit(solution)/shard_map/pallas_call | solution.py:465
  52.0 1.7 %shard_map.122 = (bf16[1,136,1024]{2,1,0:T(8,128)(2,1)}, f32[3,16,256]{2,1,0:T(8,128)}, f32[16,256]{1,0:T(8,128)}) custom-call(bf16[1,136,1024]{2,1,0:T(8,128)(2,1)} %get-tuple-element.8.block_in, f32[4,16,256]{2,1,0:T(8,128)} %get-tuple-element.9.weight_in), custom_call_target="tpu_custom_call" | custom-call | tf_op jit(solution)/shard_map/pallas_call | solution.py:475

commit v5 on v4

--- a/solution.py
+++ b/solution.py
@@ -273,16 +273,20 @@
             probs = (expd * (1.0 / total)).astype(BF16)
             r["probs"][h, at, :] = probs
             r["att"][s, :, heads[h]] = dot(probs, v).astype(BF16)
-
-    for c in range(len(pieces)):
-        u_cross[c].wait_recv()
-        u_onward[c].start()
+            if h == 1 and s >= 1:
+                u_cross[s - 1].wait_recv()
+                u_onward[s - 1].start()
+
     a_sent, a_come = new_sem(), new_sem()
     for s in (1, 2, 3):
         remote(r["att"].at[s], r["attin"].at[s - 1], peer[s], a_sent, a_come).start()
     u_near.wait_recv()
-    wait_bytes(r["ubuf"].at[3], u_onward_sem)
     for s in range(SLABS):
+        if s == 3:
+            r["ag"][pl.ds(0, 3 * PAD), :] = dot(
+                r["up"][pl.ds(0, 3 * PAD), :], r["ow"][0]
+            ).astype(BF16)
+            wait_bytes(r["ubuf"].at[3], u_onward_sem)
         at = pl.ds(s * PAD, PAD)
         up = jnp.where(r["sc_col"][at, :] < 0.0, r["ubuf"][s].astype(F32), 0.0)
         r["up"][at, :] = up.astype(BF16)
@@ -347,7 +351,8 @@
     att = jnp.concatenate([r["att"][s] for s in range(SLABS)], 0)
     first_stage((("out", 0), ("out", 1)), dot(r["up"][...], att, 0, 0))
     r["normed_t"][...] = r["normed"][...].T
-    r["ag"][...] = dot(r["up"][...], r["ow"][0]).astype(BF16)
+    last = pl.ds(3 * PAD, PAD)
+    r["ag"][last, :] = dot(r["up"][last, :], r["ow"][0]).astype(BF16)
     for h in range(2):
         r["dv"][:, heads[h]] = dot(r["probs"][h], r["ag"][:, heads[h]], 0, 0).astype(BF16)
     first_stage((("v", 0), ("v", 1)), dot(r["normed_t"][...], r["dv"][...]))

time: 53.8 us -> 53.3 us (level)
  Pallas kernels: 53.1 us -> 52.5 us
    pallas_call x1, Pallas kernels: 51.4 us -> 50.8 us  [per_device(): pl.pallas_call(functools.partial(kernel, INPUTS + OUTPUTS + tuple(buffers...]
where the time goes in v5:
time: 53.3 us; the launch traced here: 53.2 us
  Pallas kernels  52.5 us (98%)
  between operations  0.64 us (1%)
    pallas_call x1, Pallas kernels, per_device(): pl.pallas_call(functools.partial(kernel, INPUTS + OUTPUTS + tuple(buffers...  50.8 us
    pallas_call x1, Pallas kernels, per_device(): pl.pallas_call(hand_over, out_shape=(block_shape, jax.ShapeDtypeStruct((3...  1.69 us

profile of v5, /device:TPU:2, one launch (start us, length us, event | category | flops | bytes accessed | tf_op | source)
XLA Modules:
  0.0 53.2 jit_solution(16195495424528046368)
XLA Ops:
  0.6 50.8 %shard_map.121 = (bf16[1,136,1024]{2,1,0:T(8,128)(2,1)}, f32[4,16,256]{2,1,0:T(8,128)}) custom-call(f32[1,8,265]{2,1,0:T(8,128)} %refs_0_.1, bf16[1,136,1024]{2,1,0:T(8,128)(2,1)} %refs_1_.1, s32[1,521]{1,0:T(1,128)} %refs_2_.1, bf16[7,1024]{1,0:T(8,128)(2,1)} %refs_3_.1, bf16[32,1024]{1,0:T(8,128)(2,1)} %refs_4_.1, f32[1,1024]{1,0:T(1,128)} %bitcast.2, ...), custom_call_target="tpu_custom_call" | custom-call | tf_op jit(solution)/shard_map/pallas_call | solution.py:470
  51.5 1.7 %shard_map.122 = (bf16[1,136,1024]{2,1,0:T(8,128)(2,1)}, f32[3,16,256]{2,1,0:T(8,128)}, f32[16,256]{1,0:T(8,128)}) custom-call(bf16[1,136,1024]{2,1,0:T(8,128)(2,1)} %get-tuple-element.8.block_in, f32[4,16,256]{2,1,0:T(8,128)} %get-tuple-element.9.weight_in), custom_call_target="tpu_custom_call" | custom-call | tf_op jit(solution)/shard_map/pallas_call | solution.py:480

commit v6 on v5

--- a/solution.py
+++ b/solution.py
@@ -235,8 +235,8 @@
         scale = lax.rsqrt(jnp.mean(x * x, axis=-1, keepdims=True) + 1e-6)
         r["normed"][at, :] = (x * scale * r["l_norm_gain"][...]).astype(BF16)
 
-    def project(first):
-        at = pl.ds(first * PAD, 2 * PAD)
+    def project(first, count):
+        at = pl.ds(first * PAD, count * PAD)
         for b in range(3):
             r["qkv"][b, at, :] = dot(r["normed"][at, :], r["wq"][b]).astype(BF16)
 
@@ -245,7 +245,7 @@
     enter(1)
     wait_bytes(r["ow"], ow_sem)
     wait_bytes(r["wq"], wq_sem)
-    project(0)
+    project(0, 2)
     for c in range(len(pieces)):
         s_cross[c].wait_send()
         u_cross[c].start()
@@ -254,9 +254,10 @@
         s_onward[c].start()
     u_near.start()
     enter(2)
+    project(2, 1)
     wait_bytes(r["sbuf"].at[3], s_onward_sem)
     enter(3)
-    project(2)
+    project(3, 1)
 
     factor = HEAD_DIM ** (-0.5)
     heads = [slice(h * HEAD_DIM, (h + 1) * HEAD_DIM) for h in range(2)]

time: 53.3 us -> 53.5 us (level)
  no operation moved by 1% of the time
where the time goes in v6:
time: 53.5 us; the launch traced here: 53.4 us
  Pallas kernels  52.8 us (99%)
  between operations  0.64 us (1%)
    pallas_call x1, Pallas kernels, per_device(): pl.pallas_call(functools.partial(kernel, INPUTS + OUTPUTS + tuple(buffers...  51.1 us
    pallas_call x1, Pallas kernels, per_device(): pl.pallas_call(hand_over, out_shape=(block_shape, jax.ShapeDtypeStruct((3...  1.69 us

profile of v6, /device:TPU:2, one launch (start us, length us, event | category | flops | bytes accessed | tf_op | source)
XLA Modules:
  0.0 53.4 jit_solution(13044088762124616351)
XLA Ops:
  0.6 51.1 %shard_map.121 = (bf16[1,136,1024]{2,1,0:T(8,128)(2,1)}, f32[4,16,256]{2,1,0:T(8,128)}) custom-call(f32[1,8,265]{2,1,0:T(8,128)} %refs_0_.1, bf16[1,136,1024]{2,1,0:T(8,128)(2,1)} %refs_1_.1, s32[1,521]{1,0:T(1,128)} %refs_2_.1, bf16[7,1024]{1,0:T(8,128)(2,1)} %refs_3_.1, bf16[32,1024]{1,0:T(8,128)(2,1)} %refs_4_.1, f32[1,1024]{1,0:T(1,128)} %bitcast.2, ...), custom_call_target="tpu_custom_call" | custom-call | tf_op jit(solution)/shard_map/pallas_call | solution.py:471
  51.8 1.7 %shard_map.122 = (bf16[1,136,1024]{2,1,0:T(8,128)(2,1)}, f32[3,16,256]{2,1,0:T(8,128)}, f32[16,256]{1,0:T(8,128)}) custom-call(bf16[1,136,1024]{2,1,0:T(8,128)(2,1)} %get-tuple-element.8.block_in, f32[4,16,256]{2,1,0:T(8,128)} %get-tuple-element.9.weight_in), custom_call_target="tpu_custom_call" | custom-call | tf_op jit(solution)/shard_map/pallas_call | solution.py:481
